TPU v7x, 512 devices: a whole 4x4x16 slice. The times are simulated.
512 devices in a mesh: replica: 64 (over y, z_hi, x, core), dp: 8 (over z_lo).
Axes of the slice: x: 4, y: 4, z: 16 (z_hi: 2, z_lo: 8; z = z_hi * 8 + z_lo), core: 2. Of those that a mesh axis runs over, the one named last changes fastest.
Arguments:
- local_weight: float32 [2048, 8192], P(('replica', 'dp')), may hold values from -6 to 6
- adam_first: float32 [2048, 8192], P(('replica', 'dp')), may hold values from -6 to 6
- adam_second: float32 [2048, 8192], P(('replica', 'dp')), may hold values from 0.05 to 2
- hidden_acts: bfloat16 [2, 32, 65536], P(None, None, ('replica', 'dp')), may hold values from -6 to 6
- out_grads: bfloat16 [2, 65536, 8192], P(None, ('replica', 'dp')), may hold values from -0.4375 to 0.4375
- global_weight: float32 [32, 8192], P('dp', 'replica'), may hold values from -6 to 6
- outer_momentum: float32 [32, 8192], P('dp', 'replica'), may hold values from -6 to 6
Outputs:
- new_local: float32 [2048, 8192], P(('replica', 'dp'))
- new_first: float32 [2048, 8192], P(('replica', 'dp'))
- new_second: float32 [2048, 8192], P(('replica', 'dp'))
- new_global: float32 [32, 8192], P('dp', 'replica')
- new_momentum: float32 [32, 8192], P('dp', 'replica')
All inputs are finite; a program needn't handle non-finite values.
Results may differ from a plain program's by a relative error of at most 0.0003.
Values sent between devices are 32-bit elements; how exact they have to be, the bound alone decides.
No kernel may reach another device: no remote copies, remote signals or barrier semaphores. Data moves between devices by JAX's collectives and lax.ppermute only.
A program may use at most 64 MiB of HBM per device.

v0:
```python
import jax
import jax.numpy as jnp
from jax import lax
from jax.sharding import PartitionSpec as P

beta_one = 0.9
beta_two = 0.95
inner_rate = 0.02
decay_rate = 0.1
tiny_eps = 1e-08
outer_rate = 0.7
outer_beta = 0.9
mix_share = 0.5


def body(
    local_weight, adam_first, adam_second, hidden_acts, out_grads, global_weight, outer_momentum
):
    row_total = local_weight.shape[0]
    replicas = lax.axis_size("replica")
    offset = lax.axis_index("dp") * row_total
    steps_count = hidden_acts.shape[0]
    weight = local_weight
    first_moment = adam_first
    second_moment = adam_second
    gradients = []
    for inner_step in range(steps_count):
        activations = hidden_acts[inner_step]
        errors = out_grads[inner_step]
        partials = jnp.dot(activations, errors, preferred_element_type=jnp.float32)
        summed = lax.psum(partials, "dp")
        gradients.append(lax.dynamic_slice_in_dim(summed, offset, row_total, 0))
    for gradient in gradients:
        first_moment = beta_one * first_moment + (1.0 - beta_one) * gradient
        second_moment = beta_two * second_moment + (1.0 - beta_two) * gradient * gradient
        update = first_moment / (jnp.sqrt(second_moment) + tiny_eps)
        weight = weight - inner_rate * (update + decay_rate * weight)
    summed_weights = lax.psum_scatter(weight, "replica", scatter_dimension=1, tiled=True)
    average = summed_weights / replicas
    delta = global_weight - average
    new_momentum = outer_beta * outer_momentum + delta
    new_global = global_weight - outer_rate * (delta + outer_beta * new_momentum)
    gathered = lax.all_gather(new_global, "replica", axis=1, tiled=True)
    new_local = mix_share * weight + (1.0 - mix_share) * gathered
    return (new_local, first_moment, second_moment, new_global, new_momentum)


def solution(mesh):
    placed = (
        P(("replica", "dp"), None),
        P(("replica", "dp"), None),
        P(("replica", "dp"), None),
        P(None, None, ("replica", "dp")),
        P(None, ("replica", "dp"), None),
        P("dp", "replica"),
        P("dp", "replica"),
    )
    return jax.shard_map(
        body,
        mesh=mesh,
        in_specs=placed,
        out_specs=(
            P(("replica", "dp"), None),
            P(("replica", "dp"), None),
            P(("replica", "dp"), None),
            P("dp", "replica"),
            P("dp", "replica"),
        ),
        check_vma=False,
    )
```

profile of v0, /device:TPU:1, one launch (start us, length us, event | category | flops | bytes accessed | tf_op | source)
XLA Modules:
  0.0 895.0 jit_solution(9789959603347147784)
XLA Ops:
  7.2 0.0 copy-start.2
  7.2 0.0 copy-start.1
  7.2 0.0 copy-start
  7.2 0.0 all-reduce.3.cloned.1.call-start
  7.2 3.1 fusion
  10.4 3.0 fusion.2
  13.4 0.0 all-reduce.3.cloned.1.call-update
  13.4 0.0 reduce-scatter.4.cloned.1.call-start
  13.4 141.2 %all-reduce.3.cloned.1.call-done = (f32[32,8192]{1,0:T(8,128)}, f32[32,8192]{1,0:T(8,128)}) async-done(((f32[32,8192]{1,0:T(8,128)}, f32[32,8192]{1,0:T(8,128)}), (f32[32,8192]{1,0:T(8,128)}, f32[32,8192]{1,0:T(8,128)})) %all-reduce.3.cloned.1.call-update) | async-done | bytes 2097168 | tf_op jit(solution)/shard_map/psum | solution.py:31
  154.6 0.0 copy-done.2
  154.6 0.0 copy-done.1
  154.6 0.0 copy-done
  154.6 2.1 multiply_subtract_fusion
  156.8 0.0 copy-start.4
  156.8 0.0 copy-start.5
  156.8 2.6 copy.12
  159.4 0.0 reduce-scatter.4.cloned.1.call-update
  159.4 565.7 %reduce-scatter.4.cloned.1.call-done = f32[128,4]{1,0:T(8,128)} async-done(((f32[8192,4]{1,0:T(8,128)}), f32[128,4]{1,0:T(8,128)}) %reduce-scatter.4.cloned.1.call-update) | async-done | bytes 2064
  725.2 0.9 copy.13
  726.1 0.0 copy-done.4
  726.1 0.0 copy-done.5
  726.1 0.6 multiply_subtract_fusion.1
  726.7 0.0 copy-start.3
  726.7 160.8 %all_gather.3 = f32[4,8192]{1,0:T(4,128)S(1)} all-gather(f32[4,128]{1,0:T(4,128)S(1)} %get-tuple-element.7), channel_id=1, replica_groups=mesh['replica'=64,'dp'=8] {'replica'}, dimensions={1}, use_global_device_ids=true | all-gather | bytes 133120 | tf_op jit(solution)/shard_map/all_gather | solution.py:43
  887.5 0.7 add_multiply_fusion
  888.2 0.0 copy-done.3
Async XLA Ops:
  7.2 147.5 %copy-start.2 = (f32[4,8192]{1,0:T(4,128)S(1)}, f32[4,8192]{1,0:T(4,128)}, u32[]{:S(2)}) copy-start(f32[4,8192]{1,0:T(4,128)} %param.9) | copy-start | bytes 393220
  7.2 147.5 %copy-start.1 = (f32[4,8192]{1,0:T(4,128)S(1)}, f32[4,8192]{1,0:T(4,128)}, u32[]{:S(2)}) copy-start(f32[4,8192]{1,0:T(4,128)} %param.8) | copy-start | bytes 393220
  7.2 147.5 %copy-start = (f32[4,8192]{1,0:T(4,128)S(1)}, f32[4,8192]{1,0:T(4,128)}, u32[]{:S(2)}) copy-start(f32[4,8192]{1,0:T(4,128)} %param.7) | copy-start | bytes 393220
  7.2 147.4 %all-reduce.3.cloned.1.call-start = ((), (), s32[]{:S(2)}) async-start(), calls=%async_computation.2 | async-start | bytes 4194304 | tf_op jit(solution)/shard_map/psum | solution.py:31
  13.4 711.8 %reduce-scatter.4.cloned.1.call-start = ((), (), s32[]{:S(2)}) async-start(), calls=%async_computation.1 | async-start | bytes 4259840
  156.8 569.3 %copy-start.4 = (f32[4,128]{1,0:T(4,128)S(1)}, f32[4,128]{1,0:T(4,128)}, u32[]{:S(2)}) copy-start(f32[4,128]{1,0:T(4,128)} %param.12) | copy-start | bytes 6148
  156.8 569.3 %copy-start.5 = (f32[4,128]{1,0:T(4,128)S(1)}, f32[4,128]{1,0:T(4,128)}, u32[]{:S(2)}) copy-start(f32[4,128]{1,0:T(4,128)} %param.13) | copy-start | bytes 6148
  726.7 161.5 %copy-start.3 = (f32[4,128]{1,0:T(4,128)}, f32[4,128]{1,0:T(4,128)S(1)}, u32[]{:S(2)}) copy-start(f32[4,128]{1,0:T(4,128)S(1)} %get-tuple-element.7) | copy-start | bytes 6148
Sparse Core Ops, SparseCore 0:
  13.5 141.0 all-reduce.2
  159.5 565.5 reduce-scatter.3
where the time goes:
time: 895 us
  waiting for transfers between devices  707 us (79%)
  blocking collectives  161 us (18%)
  between operations  14.1 us (2%)
    unnamed x3, waiting for transfers between devices  566 us
    all_gather x1, blocking collectives, body(): gathered = lax.all_gather(new_global, 'replica', axis=1, tiled=True)  161 us
    psum x1, waiting for transfers between devices, body(): summed = lax.psum(partials, 'dp')  141 us
  transfers between devices with their start and end apart: 2, of which 2 were waited for; matrix products, arithmetic and copies ran while one was open for 0% of the time, Pallas kernels for 0%

commit v1 on v0

--- a/solution.py
+++ b/solution.py
@@ -16,31 +16,41 @@
 def body(
     local_weight, adam_first, adam_second, hidden_acts, out_grads, global_weight, outer_momentum
 ):
-    row_total = local_weight.shape[0]
     replicas = lax.axis_size("replica")
-    offset = lax.axis_index("dp") * row_total
-    steps_count = hidden_acts.shape[0]
+    rings = lax.axis_size("dp")
+    steps_count, rows, tokens = hidden_acts.shape
+    row_total = rows // rings
+    columns = out_grads.shape[2]
+    ordered = hidden_acts.reshape(steps_count, rings, row_total, tokens).transpose(1, 0, 2, 3)
+    blocks = [
+        jnp.pad(ordered[:, k : k + 1], ((0, 0), (0, 0), (0, 0), (k * tokens, (steps_count - 1 - k) * tokens)))
+        for k in range(steps_count)
+    ]
+    left = jnp.concatenate(blocks, axis=1).reshape(rings * steps_count * row_total, steps_count * tokens)
+    right = out_grads.reshape(steps_count * tokens, columns)
+    partials = jnp.dot(left, right, preferred_element_type=jnp.float32)
+    summed = lax.psum_scatter(
+        partials.reshape(rings, steps_count * row_total, columns), "dp", scatter_dimension=0, tiled=False
+    )
     weight = local_weight
     first_moment = adam_first
     second_moment = adam_second
-    gradients = []
-    for inner_step in range(steps_count):
-        activations = hidden_acts[inner_step]
-        errors = out_grads[inner_step]
-        partials = jnp.dot(activations, errors, preferred_element_type=jnp.float32)
-        summed = lax.psum(partials, "dp")
-        gradients.append(lax.dynamic_slice_in_dim(summed, offset, row_total, 0))
-    for gradient in gradients:
+    for k in range(steps_count):
+        gradient = summed[k * row_total : (k + 1) * row_total]
         first_moment = beta_one * first_moment + (1.0 - beta_one) * gradient
         second_moment = beta_two * second_moment + (1.0 - beta_two) * gradient * gradient
         update = first_moment / (jnp.sqrt(second_moment) + tiny_eps)
         weight = weight - inner_rate * (update + decay_rate * weight)
-    summed_weights = lax.psum_scatter(weight, "replica", scatter_dimension=1, tiled=True)
-    average = summed_weights / replicas
+    width = columns // replicas
+    parts = weight.reshape(row_total, replicas, width).transpose(1, 0, 2)
+    parts = lax.all_to_all(parts, "replica", 0, 0, tiled=True)
+    average = jnp.sum(parts, axis=0) / replicas
     delta = global_weight - average
     new_momentum = outer_beta * outer_momentum + delta
     new_global = global_weight - outer_rate * (delta + outer_beta * new_momentum)
-    gathered = lax.all_gather(new_global, "replica", axis=1, tiled=True)
+    copies = jnp.broadcast_to(new_global[None], (replicas, row_total, width))
+    gathered = lax.all_to_all(copies, "replica", 0, 0, tiled=True)
+    gathered = gathered.transpose(1, 0, 2).reshape(row_total, columns)
     new_local = mix_share * weight + (1.0 - mix_share) * gathered
     return (new_local, first_moment, second_moment, new_global, new_momentum)
 

time: 895 us -> 153 us (0.17)
  waiting for transfers between devices: 707 us -> 73.5 us
  blocking collectives: 161 us -> 56.5 us
    unnamed x3 -> x1, waiting for transfers between devices: 566 us -> 0.02 us
    all_gather x1 -> x0, blocking collectives: 161 us -> none  [body(): gathered = lax.all_gather(new_global, 'replica', axis=1, tiled=True)]
    psum x1 -> x0, waiting for transfers between devices: 141 us -> none  [body(): summed = lax.psum(partials, 'dp')]
    reduce_scatter x0 -> x1, waiting for transfers between devices: none -> 73.5 us  [body(): lax.psum_scatter(partials.reshape(rings, steps_count * row_total, columns...]
    all_to_all x0 -> x2, blocking collectives: none -> 56.5 us  [the longest x1 35.1 us: body(): parts = lax.all_to_all(parts, 'replica', 0, 0, tiled=True)]
  transfers between devices with their start and end apart: 2 -> 1, of which waited for: 2 -> 1; matrix products, arithmetic and copies ran while one was open for 0% -> 0% of each run, Pallas kernels for 0% -> 0%
where the time goes in v1:
time: 153 us
  waiting for transfers between devices  73.5 us (48%)
  blocking collectives  56.5 us (37%)
  between operations  14.1 us (9%)
  matrix products  4.47 us (3%)
  other arithmetic  3.47 us (2%)
    reduce_scatter x1, waiting for transfers between devices, body(): lax.psum_scatter(partials.reshape(rings, steps_count * row_total, columns...  73.5 us
    all_to_all x1, blocking collectives, body(): parts = lax.all_to_all(parts, 'replica', 0, 0, tiled=True)  35.1 us
    all_to_all x1, blocking collectives, body(): gathered = lax.all_to_all(copies, 'replica', 0, 0, tiled=True)  21.5 us
    dot_general x1, matrix products, body(): partials = jnp.dot(left, right, preferred_element_type=jnp.float32)  4.47 us
  transfers between devices with their start and end apart: 1, of which 1 were waited for; matrix products, arithmetic and copies ran while one was open for 0% of the time, Pallas kernels for 0%

profile of v1, /device:TPU:1, one launch (start us, length us, event | category | flops | bytes accessed | tf_op | source)
XLA Modules:
  0.0 152.9 jit_solution(5854807865508620468)
XLA Ops:
  7.2 0.0 reduce-scatter.2.cloned.1.call-start
  7.2 0.7 copy.16
  8.0 0.0 copy-start
  8.0 0.0 copy-start.1
  8.0 0.0 copy-start.2
  8.0 0.0 copy-start.4
  8.0 0.0 copy-start.5
  8.1 4.5 %fusion.8 = f32[8,8,8192]{2,1,0:T(8,128)} fusion(bf16[8,8,256]{2,1,0:T(8,128)(2,1)S(1)} %dot_general.5, bf16[256,8192,1]{1,0,2:T(8,128)(2,1)} %bitcast.42), kind=kOutput, calls=%fused_computation.21 | convolution fusion | flops 268435456 | bytes 6324224 | tf_op jit(solution)/shard_map/dot_general | solution.py:31
  12.5 0.0 reduce-scatter.2.cloned.1.call-update
  12.5 73.5 %reduce-scatter.2.cloned.1.call-done = f32[1,8,8192]{2,1,0:T(8,128)} async-done(((f32[8,8,8192]{2,1,0:T(8,128)}), f32[1,8,8192]{2,1,0:T(8,128)}) %reduce-scatter.2.cloned.1.call-update) | async-done | bytes 262160 | tf_op jit(solution)/shard_map/reduce_scatter | solution.py:32
  86.1 0.0 copy-done
  86.1 0.0 copy-done.1
  86.1 0.0 copy-done.2
  86.1 2.1 %multiply_subtract_fusion = (f32[4,8192]{1,0:T(4,128)S(1)}, f32[4,8192]{1,0:T(4,128)}, f32[4,8192]{1,0:T(4,128)}) fusion(f32[4,8192]{1,0:T(4,128)S(1)} %copy-done, f32[1,8,8192]{2,1,0:T(8,128)} %reduce-scatter.2.cloned.1.call-done, f32[4,8192]{1,0:T(4,128)S(1)} %copy-done.1, f32[4,8192]{1,0:T(4,128)S(1)} %copy-done.2), kind=kLoop, calls=%fused_computation.8 | loop fusion | flops 851968 | bytes 1048576 | tf_op jit(solution)/shard_map/sub | solution.py:43
  88.2 35.1 %all_to_all.10 = f32[64,4,128]{2,1,0:T(4,128)S(1)} all-to-all(f32[64,4,128]{2,1,0:T(4,128)S(1)} %bitcast.43), channel_id=1, replica_groups=mesh['replica'=64,'dp'=8] {'replica'}, dimensions={0} | all-to-all | bytes 262144 | tf_op jit(solution)/shard_map/all_to_all | solution.py:46
  123.2 0.1 reduce_sum.9
  123.3 0.0 copy-done.4
  123.3 0.0 copy-done.5
  123.3 0.6 multiply_subtract_fusion.1
  123.9 0.0 copy-start.3
  123.9 21.5 %all_to_all.11 = f32[64,4,128]{2,1,0:T(4,128)S(1)} all-to-all(f32[64,4,128]{2,1,0:T(4,128)S(1)} %broadcast_in_dim.2), channel_id=1, replica_groups=mesh['replica'=64,'dp'=8] {'replica'}, dimensions={0} | all-to-all | bytes 262144 | tf_op jit(solution)/shard_map/all_to_all | solution.py:52
  145.4 0.7 fusion.2
  146.1 0.0 copy-done.3
  (4 shorter events, 0.1 us)
Async XLA Ops:
  7.2 78.9 %reduce-scatter.2.cloned.1.call-start = ((), (), s32[]{:S(2)}) async-start(), calls=%async_computation.3 | async-start | bytes 2359296 | tf_op jit(solution)/shard_map/reduce_scatter | solution.py:32
  8.0 78.1 %copy-start = (f32[4,8192]{1,0:T(4,128)S(1)}, f32[4,8192]{1,0:T(4,128)}, u32[]{:S(2)}) copy-start(f32[4,8192]{1,0:T(4,128)} %param.7) | copy-start | bytes 393220
  8.0 78.1 %copy-start.1 = (f32[4,8192]{1,0:T(4,128)S(1)}, f32[4,8192]{1,0:T(4,128)}, u32[]{:S(2)}) copy-start(f32[4,8192]{1,0:T(4,128)} %param.8) | copy-start | bytes 393220
  8.0 78.0 %copy-start.2 = (f32[4,8192]{1,0:T(4,128)S(1)}, f32[4,8192]{1,0:T(4,128)}, u32[]{:S(2)}) copy-start(f32[4,8192]{1,0:T(4,128)} %param.9) | copy-start | bytes 393220
  8.0 115.3 %copy-start.4 = (f32[4,128]{1,0:T(4,128)S(1)}, f32[4,128]{1,0:T(4,128)}, u32[]{:S(2)}) copy-start(f32[4,128]{1,0:T(4,128)} %param.12) | copy-start | bytes 6148
  8.0 115.3 %copy-start.5 = (f32[4,128]{1,0:T(4,128)S(1)}, f32[4,128]{1,0:T(4,128)}, u32[]{:S(2)}) copy-start(f32[4,128]{1,0:T(4,128)} %param.13) | copy-start | bytes 6148
  123.9 22.2 %copy-start.3 = (f32[4,128]{1,0:T(4,128)}, f32[4,128]{1,0:T(4,128)S(1)}, u32[]{:S(2)}) copy-start(f32[4,128]{1,0:T(4,128)S(1)} %get-tuple-element.5) | copy-start | bytes 6148
Sparse Core Ops, SparseCore 0:
  12.7 73.3 reduce-scatter.1

commit v2 on v1

v2 whole, which is shorter than its diff:
```python
import jax
import jax.numpy as jnp
from jax import lax
from jax.sharding import Mesh
from jax.sharding import PartitionSpec as P

beta_one = 0.9
beta_two = 0.95
inner_rate = 0.02
decay_rate = 0.1
tiny_eps = 1e-08
outer_rate = 0.7
outer_beta = 0.9
mix_share = 0.5

REPLICA_PARTS = {"y": 4, "far": 2, "x": 4, "core": 2}
OUTER = ("y", "far")
INNER = ("x", "core")
LANES = 128


def pick(parts, index):
    return lax.dynamic_index_in_dim(parts, index, 0, keepdims=False)


def reduce_line(parts):
    size = lax.axis_size("dp")
    place = lax.axis_index("dp")
    at = lambda shift: pick(parts, lax.rem(place + shift + 2 * size, size))
    last = size - 2
    up = down = up_sent = down_sent = up_near = down_near = None
    for step in range(1, last + 1):
        hop = 1 if step < last else 2
        count = step if step < last else size - 2
        up_sent = at(-step if step < last else 2)
        if up is not None:
            up, _ = lax.optimization_barrier((up, down_sent))
            up_sent = up_sent + up
        up = lax.ppermute(up_sent, "dp", [(k, k + hop) for k in range(count)])
        down_sent = at(step if step < last else -2)
        if down is not None:
            down, _ = lax.optimization_barrier((down, up_sent))
            down_sent = down_sent + down
        down = lax.ppermute(
            down_sent, "dp", [(size - 1 - k, size - 1 - k - hop) for k in range(count)]
        )
        if step == 1:
            up_own, down_own, up_sent, down_sent = lax.optimization_barrier((at(1), at(-1), up_sent, down_sent))
            up_near = lax.ppermute(up_own, "dp", [(k, k + 1) for k in range(size - 1)])
            down_near = lax.ppermute(down_own, "dp", [(k + 1, k) for k in range(size - 1)])
    return (up + down) + (up_near + down_near) + at(0)


def copies(block, count):
    return jnp.broadcast_to(block[None], (count,) + block.shape)


def body(
    local_weight, adam_first, adam_second, hidden_acts, out_grads, global_weight, outer_momentum
):
    replicas = 1
    for size in REPLICA_PARTS.values():
        replicas *= size
    inner = REPLICA_PARTS["x"] * REPLICA_PARTS["core"]
    outer = replicas // inner
    rings = lax.axis_size("dp")
    steps_count, rows, tokens = hidden_acts.shape
    row_total = rows // rings
    columns = out_grads.shape[2]
    ordered = hidden_acts.reshape(steps_count, rings, row_total, tokens).transpose(1, 0, 2, 3)
    blocks = [
        jnp.pad(
            ordered[:, k : k + 1],
            ((0, 0), (0, 0), (0, 0), (k * tokens, (steps_count - 1 - k) * tokens)),
        )
        for k in range(steps_count)
    ]
    left = jnp.concatenate(blocks, axis=1)
    left = left.reshape(rings * steps_count * row_total, steps_count * tokens)
    right = out_grads.reshape(steps_count * tokens, columns)
    partials = jnp.dot(left, right, preferred_element_type=jnp.float32)
    summed = reduce_line(partials.reshape(rings, steps_count * row_total, columns))

    weight = local_weight
    first_moment = adam_first
    second_moment = adam_second
    for k in range(steps_count):
        gradient = summed[k * row_total : (k + 1) * row_total]
        first_moment = beta_one * first_moment + (1.0 - beta_one) * gradient
        second_moment = beta_two * second_moment + (1.0 - beta_two) * gradient * gradient
        update = first_moment / (jnp.sqrt(second_moment) + tiny_eps)
        weight = weight - inner_rate * (update + decay_rate * weight)

    pull = outer_rate * (1.0 + outer_beta)
    still = global_weight - pull * global_weight - outer_rate * outer_beta * outer_beta * outer_momentum
    slot = lax.axis_index(OUTER)
    parts = weight.reshape(row_total, outer, inner, LANES).transpose(2, 1, 0, 3)
    parts, still, slot = lax.optimization_barrier((parts, still, slot))
    parts = lax.all_to_all(parts, INNER, 0, 0, tiled=True)
    share = jnp.sum(parts, axis=0) * (pull / replicas)
    mine = lax.broadcasted_iota(jnp.int32, share.shape, 0) == slot
    share = share + jnp.where(mine, still[None], 0.0)
    shares = lax.all_to_all(copies(share, outer), OUTER, 0, 0, tiled=True)
    known = jnp.sum(shares, axis=0)
    gathered = lax.all_to_all(copies(known, inner), INNER, 0, 0, tiled=True)
    gathered, known, slot = lax.optimization_barrier((gathered, known, slot))
    gathered = gathered.transpose(2, 1, 0, 3).reshape(row_total, columns)
    new_local = mix_share * weight + (1.0 - mix_share) * gathered
    new_global = pick(known, slot)
    average = (new_global - still) * (1.0 / pull)
    new_momentum = outer_beta * outer_momentum + (global_weight - average)
    return (new_local, first_moment, second_moment, new_global, new_momentum)


def solution(mesh):
    sizes = tuple(REPLICA_PARTS.values()) + (mesh.shape["dp"],)
    fine = Mesh(mesh.devices.reshape(sizes), tuple(REPLICA_PARTS) + ("dp",))
    replica = tuple(REPLICA_PARTS)
    stacked = P(replica + ("dp",), None)
    held = P("dp", replica)
    return jax.shard_map(
        body,
        mesh=fine,
        in_specs=(
            stacked,
            stacked,
            stacked,
            P(None, None, replica + ("dp",)),
            P(None, replica + ("dp",), None),
            held,
            held,
        ),
        out_specs=(stacked, stacked, stacked, held, held),
        check_vma=False,
    )
```

time: 153 us -> 124 us (0.81)
  the two profiles are of different devices: /device:TPU:1 before, /device:TPU:128 now
where the time goes in v2:
time: 124 us; the launch traced here: 123 us
  waiting for transfers between devices  39.7 us (32%)
  blocking collectives  36.8 us (30%)
  starting transfers between devices  34.2 us (28%)
  other arithmetic  6.6 us (5%)
  matrix products  3.03 us (2%)
  local copies, waits for them, and re-layouts  1.62 us (1%)
    ppermute x6, waiting for transfers between devices, reduce_line(): lax.ppermute(down_sent, 'dp', [(size - 1 - k, size - 1 - k - hop) for k i...  29.6 us
    all_to_all x1, blocking collectives, body(): shares = lax.all_to_all(copies(share, outer), OUTER, 0, 0, tiled=True)  28.3 us
    ppermute x6, starting transfers between devices, reduce_line(): up = lax.ppermute(up_sent, 'dp', [(k, k + hop) for k in range(count)])  13 us
    ppermute x6, starting transfers between devices, reduce_line(): lax.ppermute(down_sent, 'dp', [(size - 1 - k, size - 1 - k - hop) for k i...  10.1 us
    all_to_all x1, blocking collectives, body(): gathered = lax.all_to_all(copies(known, inner), INNER, 0, 0, tiled=True)  8.52 us
    all_to_all x1, waiting for transfers between devices, body(): parts = lax.all_to_all(parts, INNER, 0, 0, tiled=True)  6.13 us
    all_to_all x1, starting transfers between devices, body(): parts = lax.all_to_all(parts, INNER, 0, 0, tiled=True)  3.99 us
    ppermute x6, waiting for transfers between devices, reduce_line(): up = lax.ppermute(up_sent, 'dp', [(k, k + hop) for k in range(count)])  3.97 us
  transfers between devices with their start and end apart: 15, of which 6 were waited for; matrix products, arithmetic and copies ran while one was open for 2% of the time, Pallas kernels for 0%

profile of v2, /device:TPU:128, one launch (start us, length us, event | category | flops | bytes accessed | tf_op | source)
XLA Modules:
  0.0 122.9 jit_solution(10301621633071987642)
XLA Ops:
  0.6 0.7 copy.35
  1.4 3.0 %fusion.9 = f32[8,8,8192]{2,1,0:T(8,128)S(1)} fusion(bf16[8,8,256]{2,1,0:T(8,128)(2,1)S(1)} %dot_general.5, bf16[256,8192,1]{1,0,2:T(8,128)(2,1)} %bitcast.51), kind=kOutput, calls=%fused_computation.37 | convolution fusion | flops 268435456 | bytes 6324224 | tf_op jit(solution)/shard_map/dot_general | solution.py:81
  4.5 1.4 %collective-permute-start = (f32[8,8192]{1,0:T(8,128)S(1)}, f32[8,8192]{1,0:T(8,128)}, u32[]{:S(2)}, u32[]{:S(2)}) collective-permute-start(f32[8,8192]{1,0:T(8,128)S(1)} %get-tuple-element.32), channel_id=1, source_target_pairs={{0,1},{8,9},{16,17},{24,25},{32,33},{40,41},{48,49},{56,57},{64,65... | collective-permute-start | bytes 786440 | tf_op jit(solution)/shard_map/ppermute | solution.py:39
  5.9 0.7 collective-permute-start.2
  6.6 3.8 %collective-permute-start.12 = (f32[8,8192]{1,0:T(8,128)S(1)}, f32[8,8192]{1,0:T(8,128)S(1)}, u32[]{:S(2)}, u32[]{:S(2)}) collective-permute-start(f32[8,8192]{1,0:T(8,128)S(1)} %get-tuple-element.31), channel_id=1, source_target_pairs={{0,1},{1,2},{2,3},{3,4},{4,5},{5,6},{6,7},{8,9},{9,10},{10,11},{11... | collective-permute-start | bytes 786440 | tf_op jit(solution)/shard_map/ppermute | solution.py:49
  10.4 3.2 %collective-permute-start.13 = (f32[8,8192]{1,0:T(8,128)S(1)}, f32[8,8192]{1,0:T(8,128)S(1)}, u32[]{:S(2)}, u32[]{:S(2)}) collective-permute-start(f32[8,8192]{1,0:T(8,128)S(1)} %get-tuple-element.32), channel_id=1, source_target_pairs={{1,0},{2,1},{3,2},{4,3},{5,4},{6,5},{7,6},{9,8},{10,9},{11,10},{12... | collective-permute-start | bytes 786440 | tf_op jit(solution)/shard_map/ppermute | solution.py:50
  13.7 1.0 bitcast_add_fusion.5
  14.7 0.7 collective-permute-start.1
  15.4 0.7 collective-permute-start.4
  16.1 0.7 collective-permute-start.3
  16.9 1.3 %collective-permute-start.6 = (f32[8,8192]{1,0:T(8,128)S(1)}, f32[8,8192]{1,0:T(8,128)S(1)}, u32[]{:S(2)}, u32[]{:S(2)}) collective-permute-start(f32[8,8192]{1,0:T(8,128)S(1)} %bitcast_add_fusion.3), channel_id=1, source_target_pairs={{7,6},{6,5},{5,4},{15,14},{14,13},{13,12},{23,22},{22,21},{21,20},... | collective-permute-start | bytes 786440 | tf_op jit(solution)/shard_map/ppermute | solution.py:44
  18.3 1.3 %collective-permute-start.5 = (f32[8,8192]{1,0:T(8,128)S(1)}, f32[8,8192]{1,0:T(8,128)S(1)}, u32[]{:S(2)}, u32[]{:S(2)}) collective-permute-start(f32[8,8192]{1,0:T(8,128)S(1)} %bitcast_add_fusion.7), channel_id=1, source_target_pairs={{0,1},{1,2},{2,3},{3,4},{8,9},{9,10},{10,11},{11,12},{16,17},{17,1... | collective-permute-start | bytes 786440 | tf_op jit(solution)/shard_map/ppermute | solution.py:39
  19.6 16.3 %collective-permute-done.6 = f32[8,8192]{1,0:T(8,128)S(1)} collective-permute-done((f32[8,8192]{1,0:T(8,128)S(1)}, f32[8,8192]{1,0:T(8,128)S(1)}, u32[]{:S(2)}, u32[]{:S(2)}) %collective-permute-start.6) | collective-permute-done | bytes 262176 | tf_op jit(solution)/shard_map/ppermute | solution.py:44
  35.9 1.9 %collective-permute-start.8 = (f32[8,8192]{1,0:T(8,128)S(1)}, f32[8,8192]{1,0:T(8,128)S(1)}, u32[]{:S(2)}, u32[]{:S(2)}) collective-permute-start(f32[8,8192]{1,0:T(8,128)S(1)} %bitcast_add_fusion.2), channel_id=1, source_target_pairs={{7,6},{6,5},{5,4},{4,3},{15,14},{14,13},{13,12},{12,11},{23,22},{2... | collective-permute-start | bytes 786440 | tf_op jit(solution)/shard_map/ppermute | solution.py:44
  37.9 4.1 %collective-permute-start.7 = (f32[8,8192]{1,0:T(8,128)S(1)}, f32[8,8192]{1,0:T(8,128)S(1)}, u32[]{:S(2)}, u32[]{:S(2)}) collective-permute-start(f32[8,8192]{1,0:T(8,128)S(1)} %bitcast_add_fusion.8), channel_id=1, source_target_pairs={{0,1},{1,2},{2,3},{3,4},{4,5},{8,9},{9,10},{10,11},{11,12},{12,13}... | collective-permute-start | bytes 786440 | tf_op jit(solution)/shard_map/ppermute | solution.py:39
  42.0 2.4 %collective-permute-done.8 = f32[8,8192]{1,0:T(8,128)S(1)} collective-permute-done((f32[8,8192]{1,0:T(8,128)S(1)}, f32[8,8192]{1,0:T(8,128)S(1)}, u32[]{:S(2)}, u32[]{:S(2)}) %collective-permute-start.8) | collective-permute-done | bytes 262176 | tf_op jit(solution)/shard_map/ppermute | solution.py:44
  44.4 3.1 %collective-permute-start.10 = (f32[8,8192]{1,0:T(8,128)S(1)}, f32[8,8192]{1,0:T(8,128)S(1)}, u32[]{:S(2)}, u32[]{:S(2)}) collective-permute-start(f32[8,8192]{1,0:T(8,128)S(1)} %bitcast_add_fusion.1), channel_id=1, source_target_pairs={{7,6},{6,5},{5,4},{4,3},{3,2},{15,14},{14,13},{13,12},{12,11},{11,... | collective-permute-start | bytes 786440 | tf_op jit(solution)/shard_map/ppermute | solution.py:44
  47.6 5.1 %collective-permute-done.10 = f32[8,8192]{1,0:T(8,128)S(1)} collective-permute-done((f32[8,8192]{1,0:T(8,128)S(1)}, f32[8,8192]{1,0:T(8,128)S(1)}, u32[]{:S(2)}, u32[]{:S(2)}) %collective-permute-start.10) | collective-permute-done | bytes 262176 | tf_op jit(solution)/shard_map/ppermute | solution.py:44
  52.7 0.7 bitcast_add_fusion.4
  53.4 2.5 %collective-permute-start.11 = (f32[8,8192]{1,0:T(8,128)}, f32[8,8192]{1,0:T(8,128)}, u32[]{:S(2)}, u32[]{:S(2)}) collective-permute-start(f32[8,8192]{1,0:T(8,128)} %bitcast_add_fusion.4), channel_id=1, source_target_pairs={{7,5},{6,4},{5,3},{4,2},{3,1},{2,0},{15,13},{14,12},{13,11},{12,10... | collective-permute-start | bytes 786440 | tf_op jit(solution)/shard_map/ppermute | solution.py:44
  55.9 4.9 %collective-permute-start.9 = (f32[8,8192]{1,0:T(8,128)S(1)}, f32[8,8192]{1,0:T(8,128)}, u32[]{:S(2)}, u32[]{:S(2)}) collective-permute-start(f32[8,8192]{1,0:T(8,128)S(1)} %bitcast_add_fusion.9), channel_id=1, source_target_pairs={{0,2},{1,3},{2,4},{3,5},{4,6},{5,7},{8,10},{9,11},{10,12},{11,13},... | collective-permute-start | bytes 786440 | tf_op jit(solution)/shard_map/ppermute | solution.py:39
  60.9 5.8 %collective-permute-done.11 = f32[8,8192]{1,0:T(8,128)} collective-permute-done((f32[8,8192]{1,0:T(8,128)}, f32[8,8192]{1,0:T(8,128)}, u32[]{:S(2)}, u32[]{:S(2)}) %collective-permute-start.11) | collective-permute-done | bytes 262176 | tf_op jit(solution)/shard_map/ppermute | solution.py:44
  66.7 3.9 %collective-permute-done.9 = f32[8,8192]{1,0:T(8,128)} collective-permute-done((f32[8,8192]{1,0:T(8,128)S(1)}, f32[8,8192]{1,0:T(8,128)}, u32[]{:S(2)}, u32[]{:S(2)}) %collective-permute-start.9) | collective-permute-done | bytes 262176 | tf_op jit(solution)/shard_map/ppermute | solution.py:39
  70.6 1.1 bitcast_add_fusion
  71.7 2.0 %multiply_subtract_fusion = (f32[4,8192]{1,0:T(4,128)S(1)}, f32[4,8192]{1,0:T(4,128)}, f32[4,8192]{1,0:T(4,128)}) fusion(f32[4,8192]{1,0:T(4,128)S(1)} %copy-done, f32[8,8192]{1,0:T(8,128)S(1)} %bitcast_add_fusion, f32[4,8192]{1,0:T(4,128)} %param.8, f32[4,8192]{1,0:T(4,128)} %param.9), kind=kLoop, calls=%fused_computation.21 | loop fusion | flops 851968 | bytes 1048576 | tf_op jit(solution)/shard_map/sub | solution.py:92
  73.7 0.7 copy.23
  74.4 4.0 %all-to-all-start = ((f32[8,8,4,128]{3,1,2,0:T(8,128)}), f32[8,8,4,128]{3,1,2,0:T(8,128)S(1)}, u32[]{:S(2)}, u32[]{:S(2)}) async-start(f32[8,8,4,128]{3,1,2,0:T(8,128)} %copy.23), calls=%async_computation | async-start | bytes 262144 | tf_op jit(solution)/shard_map/all_to_all | solution.py:99
  78.4 6.1 %all-to-all-done = f32[8,8,4,128]{3,1,2,0:T(8,128)S(1)} async-done(((f32[8,8,4,128]{3,1,2,0:T(8,128)}), f32[8,8,4,128]{3,1,2,0:T(8,128)S(1)}, u32[]{:S(2)}, u32[]{:S(2)}) %all-to-all-start) | async-done | bytes 131104 | tf_op jit(solution)/shard_map/all_to_all | solution.py:99
  84.7 28.3 %all_to_all.15 = f32[8,8,4,128]{3,1,2,0:T(8,128)S(1)} all-to-all(f32[8,8,4,128]{3,1,2,0:T(8,128)S(1)} %broadcast_in_dim.27), channel_id=1, replica_groups=mesh['y'=4,'far'=2,'x'=4,'core'=2,'dp'=8] {'y','far'}, dimensions={0} | all-to-all | bytes 262144 | tf_op jit(solution)/shard_map/all_to_all | solution.py:103
  113.0 8.5 %all_to_all.16 = f32[8,8,4,128]{3,1,2,0:T(8,128)S(1)} all-to-all(f32[8,8,4,128]{3,1,2,0:T(8,128)S(1)} %broadcast_in_dim.28), channel_id=1, replica_groups=mesh['y'=4,'far'=2,'x'=4,'core'=2,'dp'=8] {'x','core'}, dimensions={0} | all-to-all | bytes 262144 | tf_op jit(solution)/shard_map/all_to_all | solution.py:105
  121.5 0.6 subtract_add_fusion
  122.2 0.8 fusion.2
  (39 shorter events, 0.7 us)
Async XLA Ops:
  4.5 9.2 %collective-permute-start = (f32[8,8192]{1,0:T(8,128)S(1)}, f32[8,8192]{1,0:T(8,128)}, u32[]{:S(2)}, u32[]{:S(2)}) collective-permute-start(f32[8,8192]{1,0:T(8,128)S(1)} %get-tuple-element.32), channel_id=1, source_target_pairs={{0,1},{8,9},{16,17},{24,25},{32,33},{40,41},{48,49},{56,57},{64,65... | collective-permute-start | bytes 786440 | tf_op jit(solution)/shard_map/ppermute | solution.py:39
  5.9 9.5 %collective-permute-start.2 = (f32[8,8192]{1,0:T(8,128)S(1)}, f32[8,8192]{1,0:T(8,128)S(1)}, u32[]{:S(2)}, u32[]{:S(2)}) collective-permute-start(f32[8,8192]{1,0:T(8,128)S(1)} %get-tuple-element.31), channel_id=1, source_target_pairs={{7,6},{15,14},{23,22},{31,30},{39,38},{47,46},{55,54},{63,62},{71,... | collective-permute-start | bytes 786440 | tf_op jit(solution)/shard_map/ppermute | solution.py:44
  6.6 54.3 %collective-permute-start.12 = (f32[8,8192]{1,0:T(8,128)S(1)}, f32[8,8192]{1,0:T(8,128)S(1)}, u32[]{:S(2)}, u32[]{:S(2)}) collective-permute-start(f32[8,8192]{1,0:T(8,128)S(1)} %get-tuple-element.31), channel_id=1, source_target_pairs={{0,1},{1,2},{2,3},{3,4},{4,5},{5,6},{6,7},{8,9},{9,10},{10,11},{11... | collective-permute-start | bytes 786440 | tf_op jit(solution)/shard_map/ppermute | solution.py:49
  10.4 50.5 %collective-permute-start.13 = (f32[8,8192]{1,0:T(8,128)S(1)}, f32[8,8192]{1,0:T(8,128)S(1)}, u32[]{:S(2)}, u32[]{:S(2)}) collective-permute-start(f32[8,8192]{1,0:T(8,128)S(1)} %get-tuple-element.32), channel_id=1, source_target_pairs={{1,0},{2,1},{3,2},{4,3},{5,4},{6,5},{7,6},{9,8},{10,9},{11,10},{12... | collective-permute-start | bytes 786440 | tf_op jit(solution)/shard_map/ppermute | solution.py:50
  14.7 1.4 %collective-permute-start.1 = (f32[8,8192]{1,0:T(8,128)S(1)}, f32[8,8192]{1,0:T(8,128)S(1)}, u32[]{:S(2)}, u32[]{:S(2)}) collective-permute-start(f32[8,8192]{1,0:T(8,128)S(1)} %bitcast_add_fusion.5), channel_id=1, source_target_pairs={{0,1},{1,2},{8,9},{9,10},{16,17},{17,18},{24,25},{25,26},{32,33},{... | collective-permute-start | bytes 786440 | tf_op jit(solution)/shard_map/ppermute | solution.py:39
  15.4 1.4 %collective-permute-start.4 = (f32[8,8192]{1,0:T(8,128)S(1)}, f32[8,8192]{1,0:T(8,128)S(1)}, u32[]{:S(2)}, u32[]{:S(2)}) collective-permute-start(f32[8,8192]{1,0:T(8,128)S(1)} %bitcast_add_fusion.10), channel_id=1, source_target_pairs={{7,6},{6,5},{15,14},{14,13},{23,22},{22,21},{31,30},{30,29},{39,38... | collective-permute-start | bytes 786440 | tf_op jit(solution)/shard_map/ppermute | solution.py:44
  16.1 2.0 %collective-permute-start.3 = (f32[8,8192]{1,0:T(8,128)S(1)}, f32[8,8192]{1,0:T(8,128)S(1)}, u32[]{:S(2)}, u32[]{:S(2)}) collective-permute-start(f32[8,8192]{1,0:T(8,128)S(1)} %bitcast_add_fusion.6), channel_id=1, source_target_pairs={{0,1},{1,2},{2,3},{8,9},{9,10},{10,11},{16,17},{17,18},{18,19},{24... | collective-permute-start | bytes 786440 | tf_op jit(solution)/shard_map/ppermute | solution.py:39
  16.9 19.0 %collective-permute-start.6 = (f32[8,8192]{1,0:T(8,128)S(1)}, f32[8,8192]{1,0:T(8,128)S(1)}, u32[]{:S(2)}, u32[]{:S(2)}) collective-permute-start(f32[8,8192]{1,0:T(8,128)S(1)} %bitcast_add_fusion.3), channel_id=1, source_target_pairs={{7,6},{6,5},{5,4},{15,14},{14,13},{13,12},{23,22},{22,21},{21,20},... | collective-permute-start | bytes 786440 | tf_op jit(solution)/shard_map/ppermute | solution.py:44
  18.2 42.6 %copy-start.1 = (f32[4,128]{1,0:T(4,128)S(1)}, f32[4,128]{1,0:T(4,128)}, u32[]{:S(2)}) copy-start(f32[4,128]{1,0:T(4,128)} %param.12) | copy-start | bytes 6148
  18.2 42.6 %copy-start.2 = (f32[4,128]{1,0:T(4,128)S(1)}, f32[4,128]{1,0:T(4,128)}, u32[]{:S(2)}) copy-start(f32[4,128]{1,0:T(4,128)} %param.13) | copy-start | bytes 6148
  18.3 19.6 %collective-permute-start.5 = (f32[8,8192]{1,0:T(8,128)S(1)}, f32[8,8192]{1,0:T(8,128)S(1)}, u32[]{:S(2)}, u32[]{:S(2)}) collective-permute-start(f32[8,8192]{1,0:T(8,128)S(1)} %bitcast_add_fusion.7), channel_id=1, source_target_pairs={{0,1},{1,2},{2,3},{3,4},{8,9},{9,10},{10,11},{11,12},{16,17},{17,1... | collective-permute-start | bytes 786440 | tf_op jit(solution)/shard_map/ppermute | solution.py:39
  35.9 8.4 %collective-permute-start.8 = (f32[8,8192]{1,0:T(8,128)S(1)}, f32[8,8192]{1,0:T(8,128)S(1)}, u32[]{:S(2)}, u32[]{:S(2)}) collective-permute-start(f32[8,8192]{1,0:T(8,128)S(1)} %bitcast_add_fusion.2), channel_id=1, source_target_pairs={{7,6},{6,5},{5,4},{4,3},{15,14},{14,13},{13,12},{12,11},{23,22},{2... | collective-permute-start | bytes 786440 | tf_op jit(solution)/shard_map/ppermute | solution.py:44
  37.9 33.8 %copy-start = (f32[4,8192]{1,0:T(4,128)S(1)}, f32[4,8192]{1,0:T(4,128)}, u32[]{:S(2)}) copy-start(f32[4,8192]{1,0:T(4,128)} %param.7) | copy-start | bytes 393220
  37.9 9.6 %collective-permute-start.7 = (f32[8,8192]{1,0:T(8,128)S(1)}, f32[8,8192]{1,0:T(8,128)S(1)}, u32[]{:S(2)}, u32[]{:S(2)}) collective-permute-start(f32[8,8192]{1,0:T(8,128)S(1)} %bitcast_add_fusion.8), channel_id=1, source_target_pairs={{0,1},{1,2},{2,3},{3,4},{4,5},{8,9},{9,10},{10,11},{11,12},{12,13}... | collective-permute-start | bytes 786440 | tf_op jit(solution)/shard_map/ppermute | solution.py:39
  44.4 8.3 %collective-permute-start.10 = (f32[8,8192]{1,0:T(8,128)S(1)}, f32[8,8192]{1,0:T(8,128)S(1)}, u32[]{:S(2)}, u32[]{:S(2)}) collective-permute-start(f32[8,8192]{1,0:T(8,128)S(1)} %bitcast_add_fusion.1), channel_id=1, source_target_pairs={{7,6},{6,5},{5,4},{4,3},{3,2},{15,14},{14,13},{13,12},{12,11},{11,... | collective-permute-start | bytes 786440 | tf_op jit(solution)/shard_map/ppermute | solution.py:44
  53.4 13.3 %collective-permute-start.11 = (f32[8,8192]{1,0:T(8,128)}, f32[8,8192]{1,0:T(8,128)}, u32[]{:S(2)}, u32[]{:S(2)}) collective-permute-start(f32[8,8192]{1,0:T(8,128)} %bitcast_add_fusion.4), channel_id=1, source_target_pairs={{7,5},{6,4},{5,3},{4,2},{3,1},{2,0},{15,13},{14,12},{13,11},{12,10... | collective-permute-start | bytes 786440 | tf_op jit(solution)/shard_map/ppermute | solution.py:44
  55.9 14.7 %collective-permute-start.9 = (f32[8,8192]{1,0:T(8,128)S(1)}, f32[8,8192]{1,0:T(8,128)}, u32[]{:S(2)}, u32[]{:S(2)}) collective-permute-start(f32[8,8192]{1,0:T(8,128)S(1)} %bitcast_add_fusion.9), channel_id=1, source_target_pairs={{0,2},{1,3},{2,4},{3,5},{4,6},{5,7},{8,10},{9,11},{10,12},{11,13},... | collective-permute-start | bytes 786440 | tf_op jit(solution)/shard_map/ppermute | solution.py:39
  74.4 10.1 %all-to-all-start = ((f32[8,8,4,128]{3,1,2,0:T(8,128)}), f32[8,8,4,128]{3,1,2,0:T(8,128)S(1)}, u32[]{:S(2)}, u32[]{:S(2)}) async-start(f32[8,8,4,128]{3,1,2,0:T(8,128)} %copy.23), calls=%async_computation | async-start | bytes 262144 | tf_op jit(solution)/shard_map/all_to_all | solution.py:99
  121.5 1.4 %copy-start.3 = (f32[1,4,128]{2,0,1:T(1,128)}, f32[1,4,128]{2,0,1:T(1,128)S(1)}, u32[]{:S(2)}) copy-start(f32[1,4,128]{2,0,1:T(1,128)S(1)} %constant_dynamic-slice_fusion) | copy-start | bytes 6148

commit v3 on v2

--- a/solution.py
+++ b/solution.py
@@ -27,28 +27,35 @@
     size = lax.axis_size("dp")
     place = lax.axis_index("dp")
     at = lambda shift: pick(parts, lax.rem(place + shift + 2 * size, size))
+    end = size - 1
     last = size - 2
-    up = down = up_sent = down_sent = up_near = down_near = None
-    for step in range(1, last + 1):
-        hop = 1 if step < last else 2
-        count = step if step < last else size - 2
-        up_sent = at(-step if step < last else 2)
-        if up is not None:
-            up, _ = lax.optimization_barrier((up, down_sent))
-            up_sent = up_sent + up
-        up = lax.ppermute(up_sent, "dp", [(k, k + hop) for k in range(count)])
-        down_sent = at(step if step < last else -2)
-        if down is not None:
-            down, _ = lax.optimization_barrier((down, up_sent))
-            down_sent = down_sent + down
-        down = lax.ppermute(
-            down_sent, "dp", [(size - 1 - k, size - 1 - k - hop) for k in range(count)]
-        )
-        if step == 1:
-            up_own, down_own, up_sent, down_sent = lax.optimization_barrier((at(1), at(-1), up_sent, down_sent))
-            up_near = lax.ppermute(up_own, "dp", [(k, k + 1) for k in range(size - 1)])
-            down_near = lax.ppermute(down_own, "dp", [(k + 1, k) for k in range(size - 1)])
-    return (up + down) + (up_near + down_near) + at(0)
+    rights = [(k, k + 1) for k in range(end)]
+    lefts = [(k + 1, k) for k in range(end)]
+    up_sent = at(jnp.where(place == 0, end, 1))
+    down_sent = at(jnp.where(place == end, -end, -1))
+    up = lax.ppermute(up_sent, "dp", rights)
+    down = lax.ppermute(down_sent, "dp", lefts)
+    near = jnp.where(place >= 2, up, 0.0) + jnp.where(place <= end - 2, down, 0.0)
+    own = at(0) + near
+    for step in range(2, last):
+        up, _ = lax.optimization_barrier((up, down_sent))
+        up_sent = at(-step) + up
+        if step == 4:
+            up_sent, own = lax.optimization_barrier((up_sent, own))
+        up = lax.ppermute(up_sent, "dp", [(k, k + 1) for k in range(step)])
+        down, _ = lax.optimization_barrier((down, up_sent))
+        down_sent = at(step) + down
+        down = lax.ppermute(down_sent, "dp", [(end - k, end - k - 1) for k in range(step)])
+    up, _ = lax.optimization_barrier((up, down_sent))
+    up_sent = at(2) + up
+    up = lax.ppermute(up_sent, "dp", [(k, k + 2) for k in range(last)])
+    down, _ = lax.optimization_barrier((down, up_sent))
+    down_sent = at(-2) + down
+    down = lax.ppermute(down_sent, "dp", [(k + 2, k) for k in range(last)])
+    edge = at(jnp.where(place == 0, 1, -1))
+    edge, _ = lax.optimization_barrier((edge, down_sent))
+    edge = lax.ppermute(edge, "dp", [(0, 1), (end, end - 1)])
+    return (up + down) + (own + edge)
 
 
 def copies(block, count):
@@ -95,11 +102,11 @@
     still = global_weight - pull * global_weight - outer_rate * outer_beta * outer_beta * outer_momentum
     slot = lax.axis_index(OUTER)
     parts = weight.reshape(row_total, outer, inner, LANES).transpose(2, 1, 0, 3)
-    parts, still, slot = lax.optimization_barrier((parts, still, slot))
+    mine = lax.broadcasted_iota(jnp.int32, parts.shape[1:], 0) == slot
+    added = jnp.where(mine, still[None], 0.0)
+    parts, added, still, slot = lax.optimization_barrier((parts, added, still, slot))
     parts = lax.all_to_all(parts, INNER, 0, 0, tiled=True)
-    share = jnp.sum(parts, axis=0) * (pull / replicas)
-    mine = lax.broadcasted_iota(jnp.int32, share.shape, 0) == slot
-    share = share + jnp.where(mine, still[None], 0.0)
+    share = jnp.sum(parts, axis=0) * (pull / replicas) + added
     shares = lax.all_to_all(copies(share, outer), OUTER, 0, 0, tiled=True)
     known = jnp.sum(shares, axis=0)
     gathered = lax.all_to_all(copies(known, inner), INNER, 0, 0, tiled=True)

time: 124 us -> 121 us (0.976)
  the two profiles are of different devices: /device:TPU:128 before, /device:TPU:1 now
where the time goes in v3:
time: 121 us; the launch traced here: 120 us
  blocking collectives  56.7 us (47%)
  starting transfers between devices  36.6 us (30%)
  waiting for transfers between devices  18.7 us (15%)
  matrix products  3.04 us (3%)
  other arithmetic  2.97 us (2%)
    all_to_all x1, blocking collectives, body(): shares = lax.all_to_all(copies(share, outer), OUTER, 0, 0, tiled=True)  31.2 us
    ppermute x4, starting transfers between devices, reduce_line(): up = lax.ppermute(up_sent, 'dp', [(k, k + 1) for k in range(step)])  18 us
    all_to_all x1, blocking collectives, body(): parts = lax.all_to_all(parts, INNER, 0, 0, tiled=True)  15.6 us
    ppermute x4, waiting for transfers between devices, reduce_line(): up = lax.ppermute(up_sent, 'dp', [(k, k + 1) for k in range(step)])  10.4 us
    all_to_all x1, blocking collectives, body(): gathered = lax.all_to_all(copies(known, inner), INNER, 0, 0, tiled=True)  9.95 us
    ppermute x1, starting transfers between devices, reduce_line(): up = lax.ppermute(up_sent, 'dp', [(k, k + 2) for k in range(last)])  5.08 us
    ppermute x1, waiting for transfers between devices, reduce_line(): edge = lax.ppermute(edge, 'dp', [(0, 1), (end, end - 1)])  4.62 us
    ppermute x1, starting transfers between devices, reduce_line(): up = lax.ppermute(up_sent, 'dp', rights)  4.39 us
  transfers between devices with their start and end apart: 13, of which 7 were waited for; matrix products, arithmetic and copies ran while one was open for 0% of the time, Pallas kernels for 0%

profile of v3, /device:TPU:1, one launch (start us, length us, event | category | flops | bytes accessed | tf_op | source)
XLA Modules:
  0.0 120.1 jit_solution(8996863627267309053)
XLA Ops:
  0.7 0.7 copy.35
  1.5 3.0 %fusion.9 = f32[8,8,8192]{2,1,0:T(8,128)S(1)} fusion(bf16[8,8,256]{2,1,0:T(8,128)(2,1)S(1)} %dot_general.5, bf16[256,8192,1]{1,0,2:T(8,128)(2,1)} %bitcast.53), kind=kOutput, calls=%fused_computation.40 | convolution fusion | flops 268435456 | bytes 6324224 | tf_op jit(solution)/shard_map/dot_general | solution.py:88
  4.6 4.4 %collective-permute-start = (f32[8,8192]{1,0:T(8,128)S(1)}, f32[8,8192]{1,0:T(8,128)S(1)}, u32[]{:S(2)}, u32[]{:S(2)}) collective-permute-start(f32[8,8192]{1,0:T(8,128)S(1)} %get-tuple-element.50), channel_id=1, source_target_pairs={{0,1},{1,2},{2,3},{3,4},{4,5},{5,6},{6,7},{8,9},{9,10},{10,11},{11... | collective-permute-start | bytes 786440 | tf_op jit(solution)/shard_map/ppermute | solution.py:36
  9.0 1.3 %collective-permute-start.2 = (f32[8,8192]{1,0:T(8,128)S(1)}, f32[8,8192]{1,0:T(8,128)S(1)}, u32[]{:S(2)}, u32[]{:S(2)}) collective-permute-start(f32[8,8192]{1,0:T(8,128)S(1)} %get-tuple-element.49), channel_id=1, source_target_pairs={{1,0},{2,1},{3,2},{4,3},{5,4},{6,5},{7,6},{9,8},{10,9},{11,10},{12... | collective-permute-start | bytes 786440 | tf_op jit(solution)/shard_map/ppermute | solution.py:37
  10.4 1.9 %collective-permute-done = f32[8,8192]{1,0:T(8,128)S(1)} collective-permute-done((f32[8,8192]{1,0:T(8,128)S(1)}, f32[8,8192]{1,0:T(8,128)S(1)}, u32[]{:S(2)}, u32[]{:S(2)}) %collective-permute-start) | collective-permute-done | bytes 262176 | tf_op jit(solution)/shard_map/ppermute | solution.py:36
  12.3 5.2 %collective-permute-start.1 = (f32[8,8192]{1,0:T(8,128)S(1)}, f32[8,8192]{1,0:T(8,128)S(1)}, u32[]{:S(2)}, u32[]{:S(2)}) collective-permute-start(f32[8,8192]{1,0:T(8,128)S(1)} %bitcast_add_fusion.5), channel_id=1, source_target_pairs={{0,1},{1,2},{8,9},{9,10},{16,17},{17,18},{24,25},{25,26},{32,33},{... | collective-permute-start | bytes 786440 | tf_op jit(solution)/shard_map/ppermute | solution.py:45
  17.6 0.7 collective-permute-start.4
  18.3 2.5 %collective-permute-done.1 = f32[8,8192]{1,0:T(8,128)S(1)} collective-permute-done((f32[8,8192]{1,0:T(8,128)S(1)}, f32[8,8192]{1,0:T(8,128)S(1)}, u32[]{:S(2)}, u32[]{:S(2)}) %collective-permute-start.1) | collective-permute-done | bytes 262176 | tf_op jit(solution)/shard_map/ppermute | solution.py:45
  20.8 4.9 %collective-permute-start.3 = (f32[8,8192]{1,0:T(8,128)S(1)}, f32[8,8192]{1,0:T(8,128)S(1)}, u32[]{:S(2)}, u32[]{:S(2)}) collective-permute-start(f32[8,8192]{1,0:T(8,128)S(1)} %bitcast_add_fusion.6), channel_id=1, source_target_pairs={{0,1},{1,2},{2,3},{8,9},{9,10},{10,11},{16,17},{17,18},{18,19},{24... | collective-permute-start | bytes 786440 | tf_op jit(solution)/shard_map/ppermute | solution.py:45
  25.7 0.1 bitcast_add_fusion.2
  25.8 0.7 collective-permute-start.6
  26.5 2.5 %collective-permute-done.3 = f32[8,8192]{1,0:T(8,128)S(1)} collective-permute-done((f32[8,8192]{1,0:T(8,128)S(1)}, f32[8,8192]{1,0:T(8,128)S(1)}, u32[]{:S(2)}, u32[]{:S(2)}) %collective-permute-start.3) | collective-permute-done | bytes 262176 | tf_op jit(solution)/shard_map/ppermute | solution.py:45
  29.0 4.1 %collective-permute-start.5 = (f32[8,8192]{1,0:T(8,128)S(1)}, f32[8,8192]{1,0:T(8,128)S(1)}, u32[]{:S(2)}, u32[]{:S(2)}) collective-permute-start(f32[8,8192]{1,0:T(8,128)S(1)} %bitcast_add_fusion.7), channel_id=1, source_target_pairs={{0,1},{1,2},{2,3},{3,4},{8,9},{9,10},{10,11},{11,12},{16,17},{17,1... | collective-permute-start | bytes 786440 | tf_op jit(solution)/shard_map/ppermute | solution.py:45
  33.2 0.8 collective-permute-start.8
  34.1 2.4 %collective-permute-done.5 = f32[8,8192]{1,0:T(8,128)S(1)} collective-permute-done((f32[8,8192]{1,0:T(8,128)S(1)}, f32[8,8192]{1,0:T(8,128)S(1)}, u32[]{:S(2)}, u32[]{:S(2)}) %collective-permute-start.5) | collective-permute-done | bytes 262176 | tf_op jit(solution)/shard_map/ppermute | solution.py:45
  36.5 3.8 %collective-permute-start.7 = (f32[8,8192]{1,0:T(8,128)S(1)}, f32[8,8192]{1,0:T(8,128)S(1)}, u32[]{:S(2)}, u32[]{:S(2)}) collective-permute-start(f32[8,8192]{1,0:T(8,128)S(1)} %bitcast_add_fusion.8), channel_id=1, source_target_pairs={{0,1},{1,2},{2,3},{3,4},{4,5},{8,9},{9,10},{10,11},{11,12},{12,13}... | collective-permute-start | bytes 786440 | tf_op jit(solution)/shard_map/ppermute | solution.py:45
  40.4 0.7 collective-permute-start.10
  41.0 2.9 %collective-permute-done.7 = f32[8,8192]{1,0:T(8,128)S(1)} collective-permute-done((f32[8,8192]{1,0:T(8,128)S(1)}, f32[8,8192]{1,0:T(8,128)S(1)}, u32[]{:S(2)}, u32[]{:S(2)}) %collective-permute-start.7) | collective-permute-done | bytes 262176 | tf_op jit(solution)/shard_map/ppermute | solution.py:45
  44.0 5.1 %collective-permute-start.9 = (f32[8,8192]{1,0:T(8,128)S(1)}, f32[8,8192]{1,0:T(8,128)S(1)}, u32[]{:S(2)}, u32[]{:S(2)}) collective-permute-start(f32[8,8192]{1,0:T(8,128)S(1)} %bitcast_add_fusion.9), channel_id=1, source_target_pairs={{0,2},{1,3},{2,4},{3,5},{4,6},{5,7},{8,10},{9,11},{10,12},{11,13},... | collective-permute-start | bytes 786440 | tf_op jit(solution)/shard_map/ppermute | solution.py:51
  49.1 1.3 %collective-permute-start.11 = (f32[8,8192]{1,0:T(8,128)S(1)}, f32[8,8192]{1,0:T(8,128)S(1)}, u32[]{:S(2)}, u32[]{:S(2)}) collective-permute-start(f32[8,8192]{1,0:T(8,128)S(1)} %bitcast_add_fusion.4), channel_id=1, source_target_pairs={{2,0},{3,1},{4,2},{5,3},{6,4},{7,5},{10,8},{11,9},{12,10},{13,11},... | collective-permute-start | bytes 786440 | tf_op jit(solution)/shard_map/ppermute | solution.py:54
  50.4 3.7 %collective-permute-start.12 = (f32[8,8192]{1,0:T(8,128)S(1)}, f32[8,8192]{1,0:T(8,128)S(1)}, u32[]{:S(2)}, u32[]{:S(2)}) collective-permute-start(f32[8,8192]{1,0:T(8,128)S(1)} %get-tuple-element.37), channel_id=1, source_target_pairs={{0,1},{7,6},{8,9},{15,14},{16,17},{23,22},{24,25},{31,30},{32,33},... | collective-permute-start | bytes 786440 | tf_op jit(solution)/shard_map/ppermute | solution.py:57
  54.1 0.1 broadcast_select_fusion
  54.2 4.6 %collective-permute-done.12 = f32[8,8192]{1,0:T(8,128)S(1)} collective-permute-done((f32[8,8192]{1,0:T(8,128)S(1)}, f32[8,8192]{1,0:T(8,128)S(1)}, u32[]{:S(2)}, u32[]{:S(2)}) %collective-permute-start.12) | collective-permute-done | bytes 262176 | tf_op jit(solution)/shard_map/ppermute | solution.py:57
  58.8 1.8 %collective-permute-done.11 = f32[8,8192]{1,0:T(8,128)S(1)} collective-permute-done((f32[8,8192]{1,0:T(8,128)S(1)}, f32[8,8192]{1,0:T(8,128)S(1)}, u32[]{:S(2)}, u32[]{:S(2)}) %collective-permute-start.11) | collective-permute-done | bytes 262176 | tf_op jit(solution)/shard_map/ppermute | solution.py:54
  60.6 0.1 add_add_fusion
  60.7 1.1 multiply_subtract_fusion
  61.9 15.6 %all_to_all.15 = f32[8,8,4,128]{3,1,2,0:T(8,128)S(1)} all-to-all(f32[8,8,4,128]{3,1,2,0:T(8,128)S(1)} %copy.23), channel_id=1, replica_groups=mesh['y'=4,'far'=2,'x'=4,'core'=2,'dp'=8] {'x','core'}, dimensions={0} | all-to-all | bytes 262144 | tf_op jit(solution)/shard_map/all_to_all | solution.py:108
  77.5 31.2 %all_to_all.16 = f32[8,8,4,128]{3,1,2,0:T(8,128)S(1)} all-to-all(f32[8,8,4,128]{3,1,2,0:T(8,128)S(1)} %broadcast_in_dim.33), channel_id=1, replica_groups=mesh['y'=4,'far'=2,'x'=4,'core'=2,'dp'=8] {'y','far'}, dimensions={0} | all-to-all | bytes 262144 | tf_op jit(solution)/shard_map/all_to_all | solution.py:110
  108.7 9.9 %all_to_all.17 = f32[8,8,4,128]{3,1,2,0:T(8,128)S(1)} all-to-all(f32[8,8,4,128]{3,1,2,0:T(8,128)S(1)} %broadcast_in_dim.34), channel_id=1, replica_groups=mesh['y'=4,'far'=2,'x'=4,'core'=2,'dp'=8] {'x','core'}, dimensions={0} | all-to-all | bytes 262144 | tf_op jit(solution)/shard_map/all_to_all | solution.py:112
  118.7 0.1 copy.34
  118.8 0.8 fusion.2
  119.5 0.6 subtract_add_fusion
  (41 shorter events, 0.5 us)
Async XLA Ops:
  1.5 8.9 %copy-start.3 = (f32[4,128]{1,0:T(4,128)S(1)}, f32[4,128]{1,0:T(4,128)}, u32[]{:S(2)}) copy-start(f32[4,128]{1,0:T(4,128)} %param.12) | copy-start | bytes 6148
  1.5 8.9 %copy-start.4 = (f32[4,128]{1,0:T(4,128)S(1)}, f32[4,128]{1,0:T(4,128)}, u32[]{:S(2)}) copy-start(f32[4,128]{1,0:T(4,128)} %param.13) | copy-start | bytes 6148
  4.6 7.7 %collective-permute-start = (f32[8,8192]{1,0:T(8,128)S(1)}, f32[8,8192]{1,0:T(8,128)S(1)}, u32[]{:S(2)}, u32[]{:S(2)}) collective-permute-start(f32[8,8192]{1,0:T(8,128)S(1)} %get-tuple-element.50), channel_id=1, source_target_pairs={{0,1},{1,2},{2,3},{3,4},{4,5},{5,6},{6,7},{8,9},{9,10},{10,11},{11... | collective-permute-start | bytes 786440 | tf_op jit(solution)/shard_map/ppermute | solution.py:36
  9.0 8.5 %collective-permute-start.2 = (f32[8,8192]{1,0:T(8,128)S(1)}, f32[8,8192]{1,0:T(8,128)S(1)}, u32[]{:S(2)}, u32[]{:S(2)}) collective-permute-start(f32[8,8192]{1,0:T(8,128)S(1)} %get-tuple-element.49), channel_id=1, source_target_pairs={{1,0},{2,1},{3,2},{4,3},{5,4},{6,5},{7,6},{9,8},{10,9},{11,10},{12... | collective-permute-start | bytes 786440 | tf_op jit(solution)/shard_map/ppermute | solution.py:37
  12.3 8.5 %collective-permute-start.1 = (f32[8,8192]{1,0:T(8,128)S(1)}, f32[8,8192]{1,0:T(8,128)S(1)}, u32[]{:S(2)}, u32[]{:S(2)}) collective-permute-start(f32[8,8192]{1,0:T(8,128)S(1)} %bitcast_add_fusion.5), channel_id=1, source_target_pairs={{0,1},{1,2},{8,9},{9,10},{16,17},{17,18},{24,25},{25,26},{32,33},{... | collective-permute-start | bytes 786440 | tf_op jit(solution)/shard_map/ppermute | solution.py:45
  17.6 8.1 %collective-permute-start.4 = (f32[8,8192]{1,0:T(8,128)S(1)}, f32[8,8192]{1,0:T(8,128)S(1)}, u32[]{:S(2)}, u32[]{:S(2)}) collective-permute-start(f32[8,8192]{1,0:T(8,128)S(1)} %bitcast_add_fusion.10), channel_id=1, source_target_pairs={{7,6},{6,5},{15,14},{14,13},{23,22},{22,21},{31,30},{30,29},{39,38... | collective-permute-start | bytes 786440 | tf_op jit(solution)/shard_map/ppermute | solution.py:48
  20.8 8.1 %collective-permute-start.3 = (f32[8,8192]{1,0:T(8,128)S(1)}, f32[8,8192]{1,0:T(8,128)S(1)}, u32[]{:S(2)}, u32[]{:S(2)}) collective-permute-start(f32[8,8192]{1,0:T(8,128)S(1)} %bitcast_add_fusion.6), channel_id=1, source_target_pairs={{0,1},{1,2},{2,3},{8,9},{9,10},{10,11},{16,17},{17,18},{18,19},{24... | collective-permute-start | bytes 786440 | tf_op jit(solution)/shard_map/ppermute | solution.py:45
  25.8 7.4 %collective-permute-start.6 = (f32[8,8192]{1,0:T(8,128)S(1)}, f32[8,8192]{1,0:T(8,128)S(1)}, u32[]{:S(2)}, u32[]{:S(2)}) collective-permute-start(f32[8,8192]{1,0:T(8,128)S(1)} %get-tuple-element.52), channel_id=1, source_target_pairs={{7,6},{6,5},{5,4},{15,14},{14,13},{13,12},{23,22},{22,21},{21,20},... | collective-permute-start | bytes 786440 | tf_op jit(solution)/shard_map/ppermute | solution.py:48
  29.0 7.4 %collective-permute-start.5 = (f32[8,8192]{1,0:T(8,128)S(1)}, f32[8,8192]{1,0:T(8,128)S(1)}, u32[]{:S(2)}, u32[]{:S(2)}) collective-permute-start(f32[8,8192]{1,0:T(8,128)S(1)} %bitcast_add_fusion.7), channel_id=1, source_target_pairs={{0,1},{1,2},{2,3},{3,4},{8,9},{9,10},{10,11},{11,12},{16,17},{17,1... | collective-permute-start | bytes 786440 | tf_op jit(solution)/shard_map/ppermute | solution.py:45
  33.2 27.5 %copy-start = (f32[4,8192]{1,0:T(4,128)S(1)}, f32[4,8192]{1,0:T(4,128)}, u32[]{:S(2)}) copy-start(f32[4,8192]{1,0:T(4,128)} %param.7) | copy-start | bytes 393220
  33.2 27.5 %copy-start.1 = (f32[4,8192]{1,0:T(4,128)S(1)}, f32[4,8192]{1,0:T(4,128)}, u32[]{:S(2)}) copy-start(f32[4,8192]{1,0:T(4,128)} %param.8) | copy-start | bytes 393220
  33.2 27.5 %copy-start.2 = (f32[4,8192]{1,0:T(4,128)S(1)}, f32[4,8192]{1,0:T(4,128)}, u32[]{:S(2)}) copy-start(f32[4,8192]{1,0:T(4,128)} %param.9) | copy-start | bytes 393220
  33.2 7.1 %collective-permute-start.8 = (f32[8,8192]{1,0:T(8,128)S(1)}, f32[8,8192]{1,0:T(8,128)S(1)}, u32[]{:S(2)}, u32[]{:S(2)}) collective-permute-start(f32[8,8192]{1,0:T(8,128)S(1)} %bitcast_add_fusion.1), channel_id=1, source_target_pairs={{7,6},{6,5},{5,4},{4,3},{15,14},{14,13},{13,12},{12,11},{23,22},{2... | collective-permute-start | bytes 786440 | tf_op jit(solution)/shard_map/ppermute | solution.py:48
  36.5 7.5 %collective-permute-start.7 = (f32[8,8192]{1,0:T(8,128)S(1)}, f32[8,8192]{1,0:T(8,128)S(1)}, u32[]{:S(2)}, u32[]{:S(2)}) collective-permute-start(f32[8,8192]{1,0:T(8,128)S(1)} %bitcast_add_fusion.8), channel_id=1, source_target_pairs={{0,1},{1,2},{2,3},{3,4},{4,5},{8,9},{9,10},{10,11},{11,12},{12,13}... | collective-permute-start | bytes 786440 | tf_op jit(solution)/shard_map/ppermute | solution.py:45
  40.4 8.7 %collective-permute-start.10 = (f32[8,8192]{1,0:T(8,128)S(1)}, f32[8,8192]{1,0:T(8,128)S(1)}, u32[]{:S(2)}, u32[]{:S(2)}) collective-permute-start(f32[8,8192]{1,0:T(8,128)S(1)} %bitcast_add_fusion), channel_id=1, source_target_pairs={{7,6},{6,5},{5,4},{4,3},{3,2},{15,14},{14,13},{13,12},{12,11},{11,... | collective-permute-start | bytes 786440 | tf_op jit(solution)/shard_map/ppermute | solution.py:48
  44.0 16.6 %collective-permute-start.9 = (f32[8,8192]{1,0:T(8,128)S(1)}, f32[8,8192]{1,0:T(8,128)S(1)}, u32[]{:S(2)}, u32[]{:S(2)}) collective-permute-start(f32[8,8192]{1,0:T(8,128)S(1)} %bitcast_add_fusion.9), channel_id=1, source_target_pairs={{0,2},{1,3},{2,4},{3,5},{4,6},{5,7},{8,10},{9,11},{10,12},{11,13},... | collective-permute-start | bytes 786440 | tf_op jit(solution)/shard_map/ppermute | solution.py:51
  49.1 11.5 %collective-permute-start.11 = (f32[8,8192]{1,0:T(8,128)S(1)}, f32[8,8192]{1,0:T(8,128)S(1)}, u32[]{:S(2)}, u32[]{:S(2)}) collective-permute-start(f32[8,8192]{1,0:T(8,128)S(1)} %bitcast_add_fusion.4), channel_id=1, source_target_pairs={{2,0},{3,1},{4,2},{5,3},{6,4},{7,5},{10,8},{11,9},{12,10},{13,11},... | collective-permute-start | bytes 786440 | tf_op jit(solution)/shard_map/ppermute | solution.py:54
  50.4 8.4 %collective-permute-start.12 = (f32[8,8192]{1,0:T(8,128)S(1)}, f32[8,8192]{1,0:T(8,128)S(1)}, u32[]{:S(2)}, u32[]{:S(2)}) collective-permute-start(f32[8,8192]{1,0:T(8,128)S(1)} %get-tuple-element.37), channel_id=1, source_target_pairs={{0,1},{7,6},{8,9},{15,14},{16,17},{23,22},{24,25},{31,30},{32,33},... | collective-permute-start | bytes 786440 | tf_op jit(solution)/shard_map/ppermute | solution.py:57
  119.5 0.6 copy-start.5

commit v4 on v3

--- a/solution.py
+++ b/solution.py
@@ -100,20 +100,25 @@
 
     pull = outer_rate * (1.0 + outer_beta)
     still = global_weight - pull * global_weight - outer_rate * outer_beta * outer_beta * outer_momentum
-    slot = lax.axis_index(OUTER)
-    parts = weight.reshape(row_total, outer, inner, LANES).transpose(2, 1, 0, 3)
-    mine = lax.broadcasted_iota(jnp.int32, parts.shape[1:], 0) == slot
+    far = lax.axis_index("far")
+    sides = REPLICA_PARTS["far"]
+    lines = REPLICA_PARTS["y"]
+    parts = weight.reshape(row_total, lines, sides, inner, LANES).transpose(1, 3, 2, 0, 4)
+    parts = parts.reshape((lines * inner, sides) + still.shape)
+    mine = lax.broadcasted_iota(jnp.int32, parts.shape[1:], 0) == far
     added = jnp.where(mine, still[None], 0.0)
-    parts, added, still, slot = lax.optimization_barrier((parts, added, still, slot))
-    parts = lax.all_to_all(parts, INNER, 0, 0, tiled=True)
+    parts, added, still, far = lax.optimization_barrier((parts, added, still, far))
+    parts = lax.all_to_all(parts, ("y", "x", "core"), 0, 0, tiled=True)
     share = jnp.sum(parts, axis=0) * (pull / replicas) + added
-    shares = lax.all_to_all(copies(share, outer), OUTER, 0, 0, tiled=True)
-    known = jnp.sum(shares, axis=0)
-    gathered = lax.all_to_all(copies(known, inner), INNER, 0, 0, tiled=True)
-    gathered, known, slot = lax.optimization_barrier((gathered, known, slot))
-    gathered = gathered.transpose(2, 1, 0, 3).reshape(row_total, columns)
+    second = lax.ppermute(share, "far", [(0, 1)])
+    first = lax.ppermute(share, "far", [(1, 0)])
+    known = (share + second) + first
+    gathered = lax.all_to_all(copies(known, lines * inner), ("y", "x", "core"), 0, 0, tiled=True)
+    gathered, known, far = lax.optimization_barrier((gathered, known, far))
+    gathered = gathered.reshape((lines, inner, sides) + still.shape)
+    gathered = gathered.transpose(3, 0, 2, 1, 4).reshape(row_total, columns)
     new_local = mix_share * weight + (1.0 - mix_share) * gathered
-    new_global = pick(known, slot)
+    new_global = pick(known, far)
     average = (new_global - still) * (1.0 / pull)
     new_momentum = outer_beta * outer_momentum + (global_weight - average)
     return (new_local, first_moment, second_moment, new_global, new_momentum)

time: 121 us -> 114 us (0.942)
  blocking collectives: 56.7 us -> 32.9 us
  starting transfers between devices: 36.6 us -> 53 us
    all_to_all x3 -> x2, blocking collectives: 56.7 us -> 32.9 us  [the longest x1 20.8 us: body(): parts = lax.all_to_all(parts, ('y', 'x', 'core'), 0, 0, tiled=True)]
    ppermute x0 -> x2, starting transfers between devices: none -> 16.4 us  [the longest x1 15.1 us: body(): second = lax.ppermute(share, 'far', [(0, 1)])]
  transfers between devices with their start and end apart: 13 -> 15, of which waited for: 7 -> 8; matrix products, arithmetic and copies ran while one was open for 0% -> 0% of each run, Pallas kernels for 0% -> 0%
where the time goes in v4:
time: 114 us; the launch traced here: 113 us
  starting transfers between devices  53 us (46%)
  blocking collectives  32.9 us (29%)
  waiting for transfers between devices  19.4 us (17%)
  matrix products  3.04 us (3%)
  other arithmetic  3 us (3%)
    all_to_all x1, blocking collectives, body(): parts = lax.all_to_all(parts, ('y', 'x', 'core'), 0, 0, tiled=True)  20.8 us
    ppermute x4, starting transfers between devices, reduce_line(): up = lax.ppermute(up_sent, 'dp', [(k, k + 1) for k in range(step)])  18 us
    ppermute x1, starting transfers between devices, body(): second = lax.ppermute(share, 'far', [(0, 1)])  15.1 us
    all_to_all x1, blocking collectives, body(): lax.all_to_all(copies(known, lines * inner), ('y', 'x', 'core'), 0, 0, ti...  12.1 us
    ppermute x4, waiting for transfers between devices, reduce_line(): up = lax.ppermute(up_sent, 'dp', [(k, k + 1) for k in range(step)])  10.4 us
    ppermute x1, starting transfers between devices, reduce_line(): up = lax.ppermute(up_sent, 'dp', [(k, k + 2) for k in range(last)])  5.08 us
    ppermute x1, waiting for transfers between devices, reduce_line(): edge = lax.ppermute(edge, 'dp', [(0, 1), (end, end - 1)])  4.62 us
    ppermute x1, starting transfers between devices, reduce_line(): up = lax.ppermute(up_sent, 'dp', rights)  4.39 us
  transfers between devices with their start and end apart: 15, of which 8 were waited for; matrix products, arithmetic and copies ran while one was open for 0% of the time, Pallas kernels for 0%

profile of v4, /device:TPU:1, one launch (start us, length us, event | category | flops | bytes accessed | tf_op | source)
XLA Modules:
  0.0 113.4 jit_solution(14150384870433989395)
XLA Ops:
  0.7 0.7 copy.30
  1.5 3.0 %fusion.11 = f32[8,8,8192]{2,1,0:T(8,128)S(1)} fusion(bf16[8,8,256]{2,1,0:T(8,128)(2,1)S(1)} %dot_general.5, bf16[256,8192,1]{1,0,2:T(8,128)(2,1)} %bitcast.61), kind=kOutput, calls=%fused_computation.42 | convolution fusion | flops 268435456 | bytes 6324224 | tf_op jit(solution)/shard_map/dot_general | solution.py:88
  4.6 4.4 %collective-permute-start = (f32[8,8192]{1,0:T(8,128)S(1)}, f32[8,8192]{1,0:T(8,128)S(1)}, u32[]{:S(2)}, u32[]{:S(2)}) collective-permute-start(f32[8,8192]{1,0:T(8,128)S(1)} %get-tuple-element.52), channel_id=1, source_target_pairs={{0,1},{1,2},{2,3},{3,4},{4,5},{5,6},{6,7},{8,9},{9,10},{10,11},{11... | collective-permute-start | bytes 786440 | tf_op jit(solution)/shard_map/ppermute | solution.py:36
  9.0 1.3 %collective-permute-start.2 = (f32[8,8192]{1,0:T(8,128)S(1)}, f32[8,8192]{1,0:T(8,128)S(1)}, u32[]{:S(2)}, u32[]{:S(2)}) collective-permute-start(f32[8,8192]{1,0:T(8,128)S(1)} %get-tuple-element.51), channel_id=1, source_target_pairs={{1,0},{2,1},{3,2},{4,3},{5,4},{6,5},{7,6},{9,8},{10,9},{11,10},{12... | collective-permute-start | bytes 786440 | tf_op jit(solution)/shard_map/ppermute | solution.py:37
  10.4 1.9 %collective-permute-done = f32[8,8192]{1,0:T(8,128)S(1)} collective-permute-done((f32[8,8192]{1,0:T(8,128)S(1)}, f32[8,8192]{1,0:T(8,128)S(1)}, u32[]{:S(2)}, u32[]{:S(2)}) %collective-permute-start) | collective-permute-done | bytes 262176 | tf_op jit(solution)/shard_map/ppermute | solution.py:36
  12.3 5.2 %collective-permute-start.1 = (f32[8,8192]{1,0:T(8,128)S(1)}, f32[8,8192]{1,0:T(8,128)S(1)}, u32[]{:S(2)}, u32[]{:S(2)}) collective-permute-start(f32[8,8192]{1,0:T(8,128)S(1)} %bitcast_add_fusion.5), channel_id=1, source_target_pairs={{0,1},{1,2},{8,9},{9,10},{16,17},{17,18},{24,25},{25,26},{32,33},{... | collective-permute-start | bytes 786440 | tf_op jit(solution)/shard_map/ppermute | solution.py:45
  17.6 0.7 collective-permute-start.4
  18.3 2.5 %collective-permute-done.1 = f32[8,8192]{1,0:T(8,128)S(1)} collective-permute-done((f32[8,8192]{1,0:T(8,128)S(1)}, f32[8,8192]{1,0:T(8,128)S(1)}, u32[]{:S(2)}, u32[]{:S(2)}) %collective-permute-start.1) | collective-permute-done | bytes 262176 | tf_op jit(solution)/shard_map/ppermute | solution.py:45
  20.8 4.9 %collective-permute-start.3 = (f32[8,8192]{1,0:T(8,128)S(1)}, f32[8,8192]{1,0:T(8,128)S(1)}, u32[]{:S(2)}, u32[]{:S(2)}) collective-permute-start(f32[8,8192]{1,0:T(8,128)S(1)} %bitcast_add_fusion.6), channel_id=1, source_target_pairs={{0,1},{1,2},{2,3},{8,9},{9,10},{10,11},{16,17},{17,18},{18,19},{24... | collective-permute-start | bytes 786440 | tf_op jit(solution)/shard_map/ppermute | solution.py:45
  25.8 0.7 collective-permute-start.6
  26.5 2.5 %collective-permute-done.3 = f32[8,8192]{1,0:T(8,128)S(1)} collective-permute-done((f32[8,8192]{1,0:T(8,128)S(1)}, f32[8,8192]{1,0:T(8,128)S(1)}, u32[]{:S(2)}, u32[]{:S(2)}) %collective-permute-start.3) | collective-permute-done | bytes 262176 | tf_op jit(solution)/shard_map/ppermute | solution.py:45
  29.0 4.1 %collective-permute-start.5 = (f32[8,8192]{1,0:T(8,128)S(1)}, f32[8,8192]{1,0:T(8,128)S(1)}, u32[]{:S(2)}, u32[]{:S(2)}) collective-permute-start(f32[8,8192]{1,0:T(8,128)S(1)} %bitcast_add_fusion.7), channel_id=1, source_target_pairs={{0,1},{1,2},{2,3},{3,4},{8,9},{9,10},{10,11},{11,12},{16,17},{17,1... | collective-permute-start | bytes 786440 | tf_op jit(solution)/shard_map/ppermute | solution.py:45
  33.2 0.8 collective-permute-start.8
  34.1 2.4 %collective-permute-done.5 = f32[8,8192]{1,0:T(8,128)S(1)} collective-permute-done((f32[8,8192]{1,0:T(8,128)S(1)}, f32[8,8192]{1,0:T(8,128)S(1)}, u32[]{:S(2)}, u32[]{:S(2)}) %collective-permute-start.5) | collective-permute-done | bytes 262176 | tf_op jit(solution)/shard_map/ppermute | solution.py:45
  36.5 3.8 %collective-permute-start.7 = (f32[8,8192]{1,0:T(8,128)S(1)}, f32[8,8192]{1,0:T(8,128)S(1)}, u32[]{:S(2)}, u32[]{:S(2)}) collective-permute-start(f32[8,8192]{1,0:T(8,128)S(1)} %bitcast_add_fusion.8), channel_id=1, source_target_pairs={{0,1},{1,2},{2,3},{3,4},{4,5},{8,9},{9,10},{10,11},{11,12},{12,13}... | collective-permute-start | bytes 786440 | tf_op jit(solution)/shard_map/ppermute | solution.py:45
  40.4 0.7 collective-permute-start.10
  41.0 2.9 %collective-permute-done.7 = f32[8,8192]{1,0:T(8,128)S(1)} collective-permute-done((f32[8,8192]{1,0:T(8,128)S(1)}, f32[8,8192]{1,0:T(8,128)S(1)}, u32[]{:S(2)}, u32[]{:S(2)}) %collective-permute-start.7) | collective-permute-done | bytes 262176 | tf_op jit(solution)/shard_map/ppermute | solution.py:45
  44.0 5.1 %collective-permute-start.9 = (f32[8,8192]{1,0:T(8,128)S(1)}, f32[8,8192]{1,0:T(8,128)S(1)}, u32[]{:S(2)}, u32[]{:S(2)}) collective-permute-start(f32[8,8192]{1,0:T(8,128)S(1)} %bitcast_add_fusion.9), channel_id=1, source_target_pairs={{0,2},{1,3},{2,4},{3,5},{4,6},{5,7},{8,10},{9,11},{10,12},{11,13},... | collective-permute-start | bytes 786440 | tf_op jit(solution)/shard_map/ppermute | solution.py:51
  49.1 1.3 %collective-permute-start.11 = (f32[8,8192]{1,0:T(8,128)S(1)}, f32[8,8192]{1,0:T(8,128)S(1)}, u32[]{:S(2)}, u32[]{:S(2)}) collective-permute-start(f32[8,8192]{1,0:T(8,128)S(1)} %bitcast_add_fusion.4), channel_id=1, source_target_pairs={{2,0},{3,1},{4,2},{5,3},{6,4},{7,5},{10,8},{11,9},{12,10},{13,11},... | collective-permute-start | bytes 786440 | tf_op jit(solution)/shard_map/ppermute | solution.py:54
  50.4 3.7 %collective-permute-start.12 = (f32[8,8192]{1,0:T(8,128)S(1)}, f32[8,8192]{1,0:T(8,128)S(1)}, u32[]{:S(2)}, u32[]{:S(2)}) collective-permute-start(f32[8,8192]{1,0:T(8,128)S(1)} %get-tuple-element.37), channel_id=1, source_target_pairs={{0,1},{7,6},{8,9},{15,14},{16,17},{23,22},{24,25},{31,30},{32,33},... | collective-permute-start | bytes 786440 | tf_op jit(solution)/shard_map/ppermute | solution.py:57
  54.1 0.1 broadcast_select_fusion
  54.2 4.6 %collective-permute-done.12 = f32[8,8192]{1,0:T(8,128)S(1)} collective-permute-done((f32[8,8192]{1,0:T(8,128)S(1)}, f32[8,8192]{1,0:T(8,128)S(1)}, u32[]{:S(2)}, u32[]{:S(2)}) %collective-permute-start.12) | collective-permute-done | bytes 262176 | tf_op jit(solution)/shard_map/ppermute | solution.py:57
  58.8 1.8 %collective-permute-done.11 = f32[8,8192]{1,0:T(8,128)S(1)} collective-permute-done((f32[8,8192]{1,0:T(8,128)S(1)}, f32[8,8192]{1,0:T(8,128)S(1)}, u32[]{:S(2)}, u32[]{:S(2)}) %collective-permute-start.11) | collective-permute-done | bytes 262176 | tf_op jit(solution)/shard_map/ppermute | solution.py:54
  60.7 1.1 multiply_subtract_fusion
  61.8 0.1 copy.19
  61.9 20.8 %all_to_all.10 = f32[32,2,4,128]{3,2,1,0:T(4,128)S(1)} all-to-all(f32[32,2,4,128]{3,2,1,0:T(4,128)S(1)} %copy.19), channel_id=1, replica_groups=mesh['y'=4,'far'=2,'x'=4,'core'=2,'dp'=8] {'y','x','core'}, dimensions={0} | all-to-all | bytes 262144 | tf_op jit(solution)/shard_map/all_to_all | solution.py:111
  82.7 1.3 %collective-permute-start.14 = (f32[2,4,128]{2,1,0:T(4,128)S(1)}, f32[2,4,128]{2,1,0:T(4,128)S(1)}, u32[]{:S(2)}, u32[]{:S(2)}) collective-permute-start(f32[2,4,128]{2,1,0:T(4,128)S(1)} %multiply_add_fusion.2), channel_id=1, source_target_pairs={{64,0},{65,1},{66,2},{67,3},{68,4},{69,5},{70,6},{71,7},{72,8},{73... | collective-permute-start | bytes 12296 | tf_op jit(solution)/shard_map/ppermute | solution.py:114
  84.0 15.1 %collective-permute-start.13 = (f32[2,4,128]{2,1,0:T(4,128)S(1)}, f32[2,4,128]{2,1,0:T(4,128)S(1)}, u32[]{:S(2)}, u32[]{:S(2)}) collective-permute-start(f32[2,4,128]{2,1,0:T(4,128)S(1)} %multiply_add_fusion.2), channel_id=1, source_target_pairs={{0,64},{1,65},{2,66},{3,67},{4,68},{5,69},{6,70},{7,71},{8,72},{9,... | collective-permute-start | bytes 12296 | tf_op jit(solution)/shard_map/ppermute | solution.py:113
  99.1 0.7 collective-permute-done.13
  99.9 12.1 %all_to_all.11 = f32[32,2,4,128]{3,2,1,0:T(4,128)S(1)} all-to-all(f32[32,2,4,128]{3,2,1,0:T(4,128)S(1)} %broadcast_in_dim.27), channel_id=1, replica_groups=mesh['y'=4,'far'=2,'x'=4,'core'=2,'dp'=8] {'y','x','core'}, dimensions={0} | all-to-all | bytes 262144 | tf_op jit(solution)/shard_map/all_to_all | solution.py:116
  112.1 0.8 fusion.2
  112.8 0.6 subtract_add_fusion
  (42 shorter events, 0.7 us)
Async XLA Ops:
  1.5 8.9 %copy-start.3 = (f32[4,128]{1,0:T(4,128)S(1)}, f32[4,128]{1,0:T(4,128)}, u32[]{:S(2)}) copy-start(f32[4,128]{1,0:T(4,128)} %param.12) | copy-start | bytes 6148
  1.5 8.9 %copy-start.4 = (f32[4,128]{1,0:T(4,128)S(1)}, f32[4,128]{1,0:T(4,128)}, u32[]{:S(2)}) copy-start(f32[4,128]{1,0:T(4,128)} %param.13) | copy-start | bytes 6148
  4.6 7.7 %collective-permute-start = (f32[8,8192]{1,0:T(8,128)S(1)}, f32[8,8192]{1,0:T(8,128)S(1)}, u32[]{:S(2)}, u32[]{:S(2)}) collective-permute-start(f32[8,8192]{1,0:T(8,128)S(1)} %get-tuple-element.52), channel_id=1, source_target_pairs={{0,1},{1,2},{2,3},{3,4},{4,5},{5,6},{6,7},{8,9},{9,10},{10,11},{11... | collective-permute-start | bytes 786440 | tf_op jit(solution)/shard_map/ppermute | solution.py:36
  9.0 8.5 %collective-permute-start.2 = (f32[8,8192]{1,0:T(8,128)S(1)}, f32[8,8192]{1,0:T(8,128)S(1)}, u32[]{:S(2)}, u32[]{:S(2)}) collective-permute-start(f32[8,8192]{1,0:T(8,128)S(1)} %get-tuple-element.51), channel_id=1, source_target_pairs={{1,0},{2,1},{3,2},{4,3},{5,4},{6,5},{7,6},{9,8},{10,9},{11,10},{12... | collective-permute-start | bytes 786440 | tf_op jit(solution)/shard_map/ppermute | solution.py:37
  12.3 8.5 %collective-permute-start.1 = (f32[8,8192]{1,0:T(8,128)S(1)}, f32[8,8192]{1,0:T(8,128)S(1)}, u32[]{:S(2)}, u32[]{:S(2)}) collective-permute-start(f32[8,8192]{1,0:T(8,128)S(1)} %bitcast_add_fusion.5), channel_id=1, source_target_pairs={{0,1},{1,2},{8,9},{9,10},{16,17},{17,18},{24,25},{25,26},{32,33},{... | collective-permute-start | bytes 786440 | tf_op jit(solution)/shard_map/ppermute | solution.py:45
  17.6 8.1 %collective-permute-start.4 = (f32[8,8192]{1,0:T(8,128)S(1)}, f32[8,8192]{1,0:T(8,128)S(1)}, u32[]{:S(2)}, u32[]{:S(2)}) collective-permute-start(f32[8,8192]{1,0:T(8,128)S(1)} %bitcast_add_fusion.10), channel_id=1, source_target_pairs={{7,6},{6,5},{15,14},{14,13},{23,22},{22,21},{31,30},{30,29},{39,38... | collective-permute-start | bytes 786440 | tf_op jit(solution)/shard_map/ppermute | solution.py:48
  20.8 8.1 %collective-permute-start.3 = (f32[8,8192]{1,0:T(8,128)S(1)}, f32[8,8192]{1,0:T(8,128)S(1)}, u32[]{:S(2)}, u32[]{:S(2)}) collective-permute-start(f32[8,8192]{1,0:T(8,128)S(1)} %bitcast_add_fusion.6), channel_id=1, source_target_pairs={{0,1},{1,2},{2,3},{8,9},{9,10},{10,11},{16,17},{17,18},{18,19},{24... | collective-permute-start | bytes 786440 | tf_op jit(solution)/shard_map/ppermute | solution.py:45
  25.8 7.4 %collective-permute-start.6 = (f32[8,8192]{1,0:T(8,128)S(1)}, f32[8,8192]{1,0:T(8,128)S(1)}, u32[]{:S(2)}, u32[]{:S(2)}) collective-permute-start(f32[8,8192]{1,0:T(8,128)S(1)} %get-tuple-element.54), channel_id=1, source_target_pairs={{7,6},{6,5},{5,4},{15,14},{14,13},{13,12},{23,22},{22,21},{21,20},... | collective-permute-start | bytes 786440 | tf_op jit(solution)/shard_map/ppermute | solution.py:48
  29.0 7.4 %collective-permute-start.5 = (f32[8,8192]{1,0:T(8,128)S(1)}, f32[8,8192]{1,0:T(8,128)S(1)}, u32[]{:S(2)}, u32[]{:S(2)}) collective-permute-start(f32[8,8192]{1,0:T(8,128)S(1)} %bitcast_add_fusion.7), channel_id=1, source_target_pairs={{0,1},{1,2},{2,3},{3,4},{8,9},{9,10},{10,11},{11,12},{16,17},{17,1... | collective-permute-start | bytes 786440 | tf_op jit(solution)/shard_map/ppermute | solution.py:45
  33.2 27.5 %copy-start = (f32[4,8192]{1,0:T(4,128)S(1)}, f32[4,8192]{1,0:T(4,128)}, u32[]{:S(2)}) copy-start(f32[4,8192]{1,0:T(4,128)} %param.7) | copy-start | bytes 393220
  33.2 27.5 %copy-start.1 = (f32[4,8192]{1,0:T(4,128)S(1)}, f32[4,8192]{1,0:T(4,128)}, u32[]{:S(2)}) copy-start(f32[4,8192]{1,0:T(4,128)} %param.8) | copy-start | bytes 393220
  33.2 27.5 %copy-start.2 = (f32[4,8192]{1,0:T(4,128)S(1)}, f32[4,8192]{1,0:T(4,128)}, u32[]{:S(2)}) copy-start(f32[4,8192]{1,0:T(4,128)} %param.9) | copy-start | bytes 393220
  33.2 7.1 %collective-permute-start.8 = (f32[8,8192]{1,0:T(8,128)S(1)}, f32[8,8192]{1,0:T(8,128)S(1)}, u32[]{:S(2)}, u32[]{:S(2)}) collective-permute-start(f32[8,8192]{1,0:T(8,128)S(1)} %bitcast_add_fusion.1), channel_id=1, source_target_pairs={{7,6},{6,5},{5,4},{4,3},{15,14},{14,13},{13,12},{12,11},{23,22},{2... | collective-permute-start | bytes 786440 | tf_op jit(solution)/shard_map/ppermute | solution.py:48
  36.5 7.5 %collective-permute-start.7 = (f32[8,8192]{1,0:T(8,128)S(1)}, f32[8,8192]{1,0:T(8,128)S(1)}, u32[]{:S(2)}, u32[]{:S(2)}) collective-permute-start(f32[8,8192]{1,0:T(8,128)S(1)} %bitcast_add_fusion.8), channel_id=1, source_target_pairs={{0,1},{1,2},{2,3},{3,4},{4,5},{8,9},{9,10},{10,11},{11,12},{12,13}... | collective-permute-start | bytes 786440 | tf_op jit(solution)/shard_map/ppermute | solution.py:45
  40.4 8.7 %collective-permute-start.10 = (f32[8,8192]{1,0:T(8,128)S(1)}, f32[8,8192]{1,0:T(8,128)S(1)}, u32[]{:S(2)}, u32[]{:S(2)}) collective-permute-start(f32[8,8192]{1,0:T(8,128)S(1)} %bitcast_add_fusion), channel_id=1, source_target_pairs={{7,6},{6,5},{5,4},{4,3},{3,2},{15,14},{14,13},{13,12},{12,11},{11,... | collective-permute-start | bytes 786440 | tf_op jit(solution)/shard_map/ppermute | solution.py:48
  44.0 16.6 %collective-permute-start.9 = (f32[8,8192]{1,0:T(8,128)S(1)}, f32[8,8192]{1,0:T(8,128)S(1)}, u32[]{:S(2)}, u32[]{:S(2)}) collective-permute-start(f32[8,8192]{1,0:T(8,128)S(1)} %bitcast_add_fusion.9), channel_id=1, source_target_pairs={{0,2},{1,3},{2,4},{3,5},{4,6},{5,7},{8,10},{9,11},{10,12},{11,13},... | collective-permute-start | bytes 786440 | tf_op jit(solution)/shard_map/ppermute | solution.py:51
  49.1 11.5 %collective-permute-start.11 = (f32[8,8192]{1,0:T(8,128)S(1)}, f32[8,8192]{1,0:T(8,128)S(1)}, u32[]{:S(2)}, u32[]{:S(2)}) collective-permute-start(f32[8,8192]{1,0:T(8,128)S(1)} %bitcast_add_fusion.4), channel_id=1, source_target_pairs={{2,0},{3,1},{4,2},{5,3},{6,4},{7,5},{10,8},{11,9},{12,10},{13,11},... | collective-permute-start | bytes 786440 | tf_op jit(solution)/shard_map/ppermute | solution.py:54
  50.4 8.4 %collective-permute-start.12 = (f32[8,8192]{1,0:T(8,128)S(1)}, f32[8,8192]{1,0:T(8,128)S(1)}, u32[]{:S(2)}, u32[]{:S(2)}) collective-permute-start(f32[8,8192]{1,0:T(8,128)S(1)} %get-tuple-element.37), channel_id=1, source_target_pairs={{0,1},{7,6},{8,9},{15,14},{16,17},{23,22},{24,25},{31,30},{32,33},... | collective-permute-start | bytes 786440 | tf_op jit(solution)/shard_map/ppermute | solution.py:57
  82.7 16.4 %collective-permute-start.14 = (f32[2,4,128]{2,1,0:T(4,128)S(1)}, f32[2,4,128]{2,1,0:T(4,128)S(1)}, u32[]{:S(2)}, u32[]{:S(2)}) collective-permute-start(f32[2,4,128]{2,1,0:T(4,128)S(1)} %multiply_add_fusion.2), channel_id=1, source_target_pairs={{64,0},{65,1},{66,2},{67,3},{68,4},{69,5},{70,6},{71,7},{72,8},{73... | collective-permute-start | bytes 12296 | tf_op jit(solution)/shard_map/ppermute | solution.py:114
  84.0 15.8 %collective-permute-start.13 = (f32[2,4,128]{2,1,0:T(4,128)S(1)}, f32[2,4,128]{2,1,0:T(4,128)S(1)}, u32[]{:S(2)}, u32[]{:S(2)}) collective-permute-start(f32[2,4,128]{2,1,0:T(4,128)S(1)} %multiply_add_fusion.2), channel_id=1, source_target_pairs={{0,64},{1,65},{2,66},{3,67},{4,68},{5,69},{6,70},{7,71},{8,72},{9,... | collective-permute-start | bytes 12296 | tf_op jit(solution)/shard_map/ppermute | solution.py:113

commit v5 on v4

--- a/solution.py
+++ b/solution.py
@@ -1,6 +1,10 @@
+import functools
+
 import jax
 import jax.numpy as jnp
 from jax import lax
+from jax.experimental import pallas as pl
+from jax.experimental.pallas import tpu as pltpu
 from jax.sharding import Mesh
 from jax.sharding import PartitionSpec as P
 
@@ -21,6 +25,66 @@
 
 def pick(parts, index):
     return lax.dynamic_index_in_dim(parts, index, 0, keepdims=False)
+
+
+CHUNKS = 2
+
+
+def partial_kernel(rings, hidden_hbm, grads_hbm, out_ref, hidden, grads, hidden_sem, grads_sem):
+    steps, rows, tokens = hidden.shape
+    width = grads.shape[3]
+    held = rows // rings
+    group = steps * held
+    total = rings * group
+    hidden_copy = pltpu.make_async_copy(hidden_hbm, hidden, hidden_sem)
+    hidden_copy.start()
+    fetches = []
+    for part in range(CHUNKS):
+        fetch = pltpu.make_async_copy(
+            grads_hbm.at[:, :, pl.ds(part * width, width)], grads.at[part], grads_sem.at[part]
+        )
+        fetch.start()
+        fetches.append(fetch)
+    place = lax.broadcasted_iota(jnp.int32, (total, rows), 0)
+    source = lax.broadcasted_iota(jnp.int32, (total, rows), 1)
+    choices = []
+    for k in range(steps):
+        wanted = (place // group) * held + place % group - k * held
+        chosen = (source == wanted) & ((place % group) // held == k)
+        choices.append(jnp.where(chosen, 1.0, 0.0).astype(jnp.bfloat16))
+    hidden_copy.wait()
+    blocks = [
+        jnp.dot(choices[k], hidden[k], preferred_element_type=jnp.float32).astype(jnp.bfloat16)
+        for k in range(steps)
+    ]
+    left = jnp.concatenate(blocks, axis=1)
+    for part in range(CHUNKS):
+        fetches[part].wait()
+        right = grads[part].reshape(steps * tokens, width)
+        product = jnp.dot(left, right, preferred_element_type=jnp.float32)
+        out_ref[:, :, part * width : (part + 1) * width] = product.reshape(rings, group, width)
+
+
+def partial_gradients(hidden_acts, out_grads, rings):
+    steps, rows, tokens = hidden_acts.shape
+    columns = out_grads.shape[2]
+    return pl.pallas_call(
+        functools.partial(partial_kernel, rings),
+        out_shape=jax.ShapeDtypeStruct((rings, steps * rows // rings, columns), jnp.float32),
+        in_specs=[pl.BlockSpec(memory_space=pltpu.HBM)] * 2,
+        out_specs=pl.BlockSpec(memory_space=pltpu.VMEM),
+        scratch_shapes=[
+            pltpu.VMEM(hidden_acts.shape, hidden_acts.dtype),
+            pltpu.VMEM((CHUNKS, steps, tokens, columns // CHUNKS), out_grads.dtype),
+            pltpu.SemaphoreType.DMA,
+            pltpu.SemaphoreType.DMA((CHUNKS,)),
+        ],
+        compiler_params=pltpu.CompilerParams(vmem_limit_bytes=24 * 1024 * 1024),
+        name="partial_gradients",
+    )(
+        pltpu.with_memory_space_constraint(hidden_acts, pltpu.HBM),
+        pltpu.with_memory_space_constraint(out_grads, pltpu.HBM),
+    )
 
 
 def reduce_line(parts):
@@ -46,15 +110,15 @@
         down, _ = lax.optimization_barrier((down, up_sent))
         down_sent = at(step) + down
         down = lax.ppermute(down_sent, "dp", [(end - k, end - k - 1) for k in range(step)])
+        if step == 5:
+            edge, _ = lax.optimization_barrier((at(jnp.where(place == 0, 1, -1)), down_sent))
+            edge = lax.ppermute(edge, "dp", [(0, 1), (end, end - 1)])
     up, _ = lax.optimization_barrier((up, down_sent))
     up_sent = at(2) + up
     up = lax.ppermute(up_sent, "dp", [(k, k + 2) for k in range(last)])
     down, _ = lax.optimization_barrier((down, up_sent))
     down_sent = at(-2) + down
     down = lax.ppermute(down_sent, "dp", [(k + 2, k) for k in range(last)])
-    edge = at(jnp.where(place == 0, 1, -1))
-    edge, _ = lax.optimization_barrier((edge, down_sent))
-    edge = lax.ppermute(edge, "dp", [(0, 1), (end, end - 1)])
     return (up + down) + (own + edge)
 
 
@@ -71,22 +135,9 @@
     inner = REPLICA_PARTS["x"] * REPLICA_PARTS["core"]
     outer = replicas // inner
     rings = lax.axis_size("dp")
-    steps_count, rows, tokens = hidden_acts.shape
-    row_total = rows // rings
-    columns = out_grads.shape[2]
-    ordered = hidden_acts.reshape(steps_count, rings, row_total, tokens).transpose(1, 0, 2, 3)
-    blocks = [
-        jnp.pad(
-            ordered[:, k : k + 1],
-            ((0, 0), (0, 0), (0, 0), (k * tokens, (steps_count - 1 - k) * tokens)),
-        )
-        for k in range(steps_count)
-    ]
-    left = jnp.concatenate(blocks, axis=1)
-    left = left.reshape(rings * steps_count * row_total, steps_count * tokens)
-    right = out_grads.reshape(steps_count * tokens, columns)
-    partials = jnp.dot(left, right, preferred_element_type=jnp.float32)
-    summed = reduce_line(partials.reshape(rings, steps_count * row_total, columns))
+    steps_count = hidden_acts.shape[0]
+    row_total, columns = local_weight.shape
+    summed = reduce_line(partial_gradients(hidden_acts, out_grads, rings))
 
     weight = local_weight
     first_moment = adam_first
@@ -110,17 +161,17 @@
     parts, added, still, far = lax.optimization_barrier((parts, added, still, far))
     parts = lax.all_to_all(parts, ("y", "x", "core"), 0, 0, tiled=True)
     share = jnp.sum(parts, axis=0) * (pull / replicas) + added
-    second = lax.ppermute(share, "far", [(0, 1)])
-    first = lax.ppermute(share, "far", [(1, 0)])
-    known = (share + second) + first
-    gathered = lax.all_to_all(copies(known, lines * inner), ("y", "x", "core"), 0, 0, tiled=True)
-    gathered, known, far = lax.optimization_barrier((gathered, known, far))
+    known = share + lax.ppermute(share, "far", [(0, 1), (1, 0)])
+    new_global = pick(known, far)
+    average = (new_global - still) * (1.0 / pull)
+    new_momentum = outer_beta * outer_momentum + (global_weight - average)
+    sent, new_global, new_momentum = lax.optimization_barrier(
+        (copies(known, lines * inner), new_global, new_momentum)
+    )
+    gathered = lax.all_to_all(sent, ("y", "x", "core"), 0, 0, tiled=True)
     gathered = gathered.reshape((lines, inner, sides) + still.shape)
     gathered = gathered.transpose(3, 0, 2, 1, 4).reshape(row_total, columns)
     new_local = mix_share * weight + (1.0 - mix_share) * gathered
-    new_global = pick(known, far)
-    average = (new_global - still) * (1.0 / pull)
-    new_momentum = outer_beta * outer_momentum + (global_weight - average)
     return (new_local, first_moment, second_moment, new_global, new_momentum)
 
 

time: 114 us -> 111 us (0.974)
  starting transfers between devices: 53 us -> 48.7 us
  matrix products: 3.04 us -> 0 us
  waiting for transfers between devices: 19.4 us -> 22.4 us
  Pallas kernels: 0 us -> 2.76 us
    ppermute x1, waiting for transfers between devices: 1.81 us -> 12 us  [reduce_line(): down = lax.ppermute(down_sent, 'dp', [(k + 2, k) for k in range(last)])]
    ppermute x1, waiting for transfers between devices: 4.62 us -> 0.01 us  [reduce_line(): edge = lax.ppermute(edge, 'dp', [(0, 1), (end, end - 1)])]
    ppermute x2 -> x1, starting transfers between devices: 16.4 us -> 12.9 us  [body(): known = share + lax.ppermute(share, 'far', [(0, 1), (1, 0)])]
    dot_general x1 -> x0, matrix products: 3.04 us -> none  [body(): partials = jnp.dot(left, right, preferred_element_type=jnp.float32)]
    ppermute x4, waiting for transfers between devices: 10.4 us -> 7.44 us  [reduce_line(): up = lax.ppermute(up_sent, 'dp', [(k, k + 1) for k in range(step)])]
    pallas_call x0 -> x1, Pallas kernels: none -> 2.76 us  [partial_gradients(): pl.pallas_call(functools.partial(partial_kernel, rings), out_shape=jax.Sh...]
  transfers between devices with their start and end apart: 15 -> 14, of which waited for: 8 -> 6; matrix products, arithmetic and copies ran while one was open for 0% -> 0% of each run, Pallas kernels for 0% -> 0%
where the time goes in v5:
time: 111 us
  starting transfers between devices  48.7 us (44%)
  blocking collectives  32.8 us (30%)
  waiting for transfers between devices  22.4 us (20%)
  other arithmetic  2.99 us (3%)
  Pallas kernels  2.76 us (2%)
    all_to_all x1, blocking collectives, body(): parts = lax.all_to_all(parts, ('y', 'x', 'core'), 0, 0, tiled=True)  20.7 us
    ppermute x4, starting transfers between devices, reduce_line(): up = lax.ppermute(up_sent, 'dp', [(k, k + 1) for k in range(step)])  18 us
    ppermute x1, starting transfers between devices, body(): known = share + lax.ppermute(share, 'far', [(0, 1), (1, 0)])  12.9 us
    all_to_all x1, blocking collectives, body(): gathered = lax.all_to_all(sent, ('y', 'x', 'core'), 0, 0, tiled=True)  12.1 us
    ppermute x1, waiting for transfers between devices, reduce_line(): down = lax.ppermute(down_sent, 'dp', [(k + 2, k) for k in range(last)])  12 us
    ppermute x4, waiting for transfers between devices, reduce_line(): up = lax.ppermute(up_sent, 'dp', [(k, k + 1) for k in range(step)])  7.44 us
    ppermute x1, starting transfers between devices, reduce_line(): up = lax.ppermute(up_sent, 'dp', rights)  4.39 us
    ppermute x1, starting transfers between devices, reduce_line(): up = lax.ppermute(up_sent, 'dp', [(k, k + 2) for k in range(last)])  4.16 us
  transfers between devices with their start and end apart: 14, of which 6 were waited for; matrix products, arithmetic and copies ran while one was open for 0% of the time, Pallas kernels for 0%

profile of v5, /device:TPU:1, one launch (start us, length us, event | category | flops | bytes accessed | tf_op | source)
XLA Modules:
  0.0 111.0 jit_solution(111135835990284563)
XLA Ops:
  0.7 2.8 %partial_gradients.1 = f32[8,8,8192]{2,1,0:T(8,128)S(1)} custom-call(bf16[2,32,128]{2,1,0:T(8,128)(2,1)} %hidden_hbm.1, bf16[2,128,8192]{2,1,0:T(8,128)(2,1)} %grads_hbm.1), custom_call_target="tpu_custom_call" | custom-call | tf_op jit(solution)/shard_map/partial_gradients/pallas_call | solution.py:71
  3.5 0.1 dynamic-slice_bitcast_fusion
  3.5 4.4 %collective-permute-start = (f32[8,8192]{1,0:T(8,128)S(1)}, f32[8,8192]{1,0:T(8,128)S(1)}, u32[]{:S(2)}, u32[]{:S(2)}) collective-permute-start(f32[8,8192]{1,0:T(8,128)S(1)} %get-tuple-element.52), channel_id=1, source_target_pairs={{0,1},{1,2},{2,3},{3,4},{4,5},{5,6},{6,7},{8,9},{9,10},{10,11},{11... | collective-permute-start | bytes 786440 | tf_op jit(solution)/shard_map/ppermute | solution.py:100
  7.9 1.3 %collective-permute-start.2 = (f32[8,8192]{1,0:T(8,128)S(1)}, f32[8,8192]{1,0:T(8,128)S(1)}, u32[]{:S(2)}, u32[]{:S(2)}) collective-permute-start(f32[8,8192]{1,0:T(8,128)S(1)} %get-tuple-element.51), channel_id=1, source_target_pairs={{1,0},{2,1},{3,2},{4,3},{5,4},{6,5},{7,6},{9,8},{10,9},{11,10},{12... | collective-permute-start | bytes 786440 | tf_op jit(solution)/shard_map/ppermute | solution.py:101
  9.3 1.9 %collective-permute-done = f32[8,8192]{1,0:T(8,128)S(1)} collective-permute-done((f32[8,8192]{1,0:T(8,128)S(1)}, f32[8,8192]{1,0:T(8,128)S(1)}, u32[]{:S(2)}, u32[]{:S(2)}) %collective-permute-start) | collective-permute-done | bytes 262176 | tf_op jit(solution)/shard_map/ppermute | solution.py:100
  11.2 5.2 %collective-permute-start.1 = (f32[8,8192]{1,0:T(8,128)S(1)}, f32[8,8192]{1,0:T(8,128)S(1)}, u32[]{:S(2)}, u32[]{:S(2)}) collective-permute-start(f32[8,8192]{1,0:T(8,128)S(1)} %bitcast_add_fusion.5), channel_id=1, source_target_pairs={{0,1},{1,2},{8,9},{9,10},{16,17},{17,18},{24,25},{25,26},{32,33},{... | collective-permute-start | bytes 786440 | tf_op jit(solution)/shard_map/ppermute | solution.py:109
  16.5 0.7 collective-permute-start.4
  17.2 2.5 %collective-permute-done.1 = f32[8,8192]{1,0:T(8,128)S(1)} collective-permute-done((f32[8,8192]{1,0:T(8,128)S(1)}, f32[8,8192]{1,0:T(8,128)S(1)}, u32[]{:S(2)}, u32[]{:S(2)}) %collective-permute-start.1) | collective-permute-done | bytes 262176 | tf_op jit(solution)/shard_map/ppermute | solution.py:109
  19.8 4.9 %collective-permute-start.3 = (f32[8,8192]{1,0:T(8,128)S(1)}, f32[8,8192]{1,0:T(8,128)S(1)}, u32[]{:S(2)}, u32[]{:S(2)}) collective-permute-start(f32[8,8192]{1,0:T(8,128)S(1)} %bitcast_add_fusion.6), channel_id=1, source_target_pairs={{0,1},{1,2},{2,3},{8,9},{9,10},{10,11},{16,17},{17,18},{18,19},{24... | collective-permute-start | bytes 786440 | tf_op jit(solution)/shard_map/ppermute | solution.py:109
  24.6 0.1 bitcast_add_fusion.2
  24.7 0.7 collective-permute-start.6
  25.4 2.5 %collective-permute-done.3 = f32[8,8192]{1,0:T(8,128)S(1)} collective-permute-done((f32[8,8192]{1,0:T(8,128)S(1)}, f32[8,8192]{1,0:T(8,128)S(1)}, u32[]{:S(2)}, u32[]{:S(2)}) %collective-permute-start.3) | collective-permute-done | bytes 262176 | tf_op jit(solution)/shard_map/ppermute | solution.py:109
  28.0 4.1 %collective-permute-start.5 = (f32[8,8192]{1,0:T(8,128)S(1)}, f32[8,8192]{1,0:T(8,128)S(1)}, u32[]{:S(2)}, u32[]{:S(2)}) collective-permute-start(f32[8,8192]{1,0:T(8,128)S(1)} %bitcast_add_fusion.7), channel_id=1, source_target_pairs={{0,1},{1,2},{2,3},{3,4},{8,9},{9,10},{10,11},{11,12},{16,17},{17,1... | collective-permute-start | bytes 786440 | tf_op jit(solution)/shard_map/ppermute | solution.py:109
  32.1 0.0 copy-start
  32.2 0.8 collective-permute-start.8
  33.0 2.4 %collective-permute-done.5 = f32[8,8192]{1,0:T(8,128)S(1)} collective-permute-done((f32[8,8192]{1,0:T(8,128)S(1)}, f32[8,8192]{1,0:T(8,128)S(1)}, u32[]{:S(2)}, u32[]{:S(2)}) %collective-permute-start.5) | collective-permute-done | bytes 262176 | tf_op jit(solution)/shard_map/ppermute | solution.py:109
  35.4 3.8 %collective-permute-start.7 = (f32[8,8192]{1,0:T(8,128)S(1)}, f32[8,8192]{1,0:T(8,128)S(1)}, u32[]{:S(2)}, u32[]{:S(2)}) collective-permute-start(f32[8,8192]{1,0:T(8,128)S(1)} %bitcast_add_fusion.8), channel_id=1, source_target_pairs={{0,1},{1,2},{2,3},{3,4},{4,5},{8,9},{9,10},{10,11},{11,12},{12,13}... | collective-permute-start | bytes 786440 | tf_op jit(solution)/shard_map/ppermute | solution.py:109
  39.3 0.7 collective-permute-start.10
  40.0 3.8 %collective-permute-start.12 = (f32[8,8192]{1,0:T(8,128)S(1)}, f32[8,8192]{1,0:T(8,128)S(1)}, u32[]{:S(2)}, u32[]{:S(2)}) collective-permute-start(f32[8,8192]{1,0:T(8,128)S(1)} %get-tuple-element.37), channel_id=1, source_target_pairs={{0,1},{7,6},{8,9},{15,14},{16,17},{23,22},{24,25},{31,30},{32,33},... | collective-permute-start | bytes 786440 | tf_op jit(solution)/shard_map/ppermute | solution.py:115
  43.8 4.2 %collective-permute-start.9 = (f32[8,8192]{1,0:T(8,128)S(1)}, f32[8,8192]{1,0:T(8,128)S(1)}, u32[]{:S(2)}, u32[]{:S(2)}) collective-permute-start(f32[8,8192]{1,0:T(8,128)S(1)} %bitcast_add_fusion.9), channel_id=1, source_target_pairs={{0,2},{1,3},{2,4},{3,5},{4,6},{5,7},{8,10},{9,11},{10,12},{11,13},... | collective-permute-start | bytes 786440 | tf_op jit(solution)/shard_map/ppermute | solution.py:118
  48.1 1.3 %collective-permute-start.11 = (f32[8,8192]{1,0:T(8,128)S(1)}, f32[8,8192]{1,0:T(8,128)S(1)}, u32[]{:S(2)}, u32[]{:S(2)}) collective-permute-start(f32[8,8192]{1,0:T(8,128)S(1)} %bitcast_add_fusion.4), channel_id=1, source_target_pairs={{2,0},{3,1},{4,2},{5,3},{6,4},{7,5},{10,8},{11,9},{12,10},{13,11},... | collective-permute-start | bytes 786440 | tf_op jit(solution)/shard_map/ppermute | solution.py:121
  49.4 0.1 broadcast_select_fusion
  49.4 12.0 %collective-permute-done.11 = f32[8,8192]{1,0:T(8,128)S(1)} collective-permute-done((f32[8,8192]{1,0:T(8,128)S(1)}, f32[8,8192]{1,0:T(8,128)S(1)}, u32[]{:S(2)}, u32[]{:S(2)}) %collective-permute-start.11) | collective-permute-done | bytes 262176 | tf_op jit(solution)/shard_map/ppermute | solution.py:121
  61.5 0.1 add_add_fusion
  61.6 1.1 multiply_subtract_fusion
  62.7 0.1 copy.15
  62.8 20.7 %all_to_all.10 = f32[32,2,4,128]{3,2,1,0:T(4,128)S(1)} all-to-all(f32[32,2,4,128]{3,2,1,0:T(4,128)S(1)} %copy.15), channel_id=1, replica_groups=mesh['y'=4,'far'=2,'x'=4,'core'=2,'dp'=8] {'y','x','core'}, dimensions={0} | all-to-all | bytes 262144 | tf_op jit(solution)/shard_map/all_to_all | solution.py:162
  83.5 12.9 %collective-permute-start.13 = (f32[2,4,128]{2,1,0:T(4,128)S(1)}, f32[2,4,128]{2,1,0:T(4,128)S(1)}, u32[]{:S(2)}, u32[]{:S(2)}) collective-permute-start(f32[2,4,128]{2,1,0:T(4,128)S(1)} %multiply_add_fusion.2), channel_id=1, source_target_pairs={{0,64},{64,0},{1,65},{65,1},{2,66},{66,2},{3,67},{67,3},{4,68},{68... | collective-permute-start | bytes 12296 | tf_op jit(solution)/shard_map/ppermute | solution.py:164
  96.4 1.0 collective-permute-done.13
  97.4 0.6 subtract_add_fusion
  98.0 12.1 %all_to_all.11 = f32[32,2,4,128]{3,2,1,0:T(4,128)S(1)} all-to-all(f32[32,2,4,128]{3,2,1,0:T(4,128)S(1)} %broadcast_in_dim.27), channel_id=1, replica_groups=mesh['y'=4,'far'=2,'x'=4,'core'=2,'dp'=8] {'y','x','core'}, dimensions={0} | all-to-all | bytes 262144 | tf_op jit(solution)/shard_map/all_to_all | solution.py:171
  110.2 0.8 fusion.2
  (36 shorter events, 0.5 us)
Async XLA Ops:
  0.7 8.6 %copy-start.3 = (f32[4,128]{1,0:T(4,128)S(1)}, f32[4,128]{1,0:T(4,128)}, u32[]{:S(2)}) copy-start(f32[4,128]{1,0:T(4,128)} %param.12) | copy-start | bytes 6148
  0.7 8.6 %copy-start.4 = (f32[4,128]{1,0:T(4,128)S(1)}, f32[4,128]{1,0:T(4,128)}, u32[]{:S(2)}) copy-start(f32[4,128]{1,0:T(4,128)} %param.13) | copy-start | bytes 6148
  3.5 7.7 %collective-permute-start = (f32[8,8192]{1,0:T(8,128)S(1)}, f32[8,8192]{1,0:T(8,128)S(1)}, u32[]{:S(2)}, u32[]{:S(2)}) collective-permute-start(f32[8,8192]{1,0:T(8,128)S(1)} %get-tuple-element.52), channel_id=1, source_target_pairs={{0,1},{1,2},{2,3},{3,4},{4,5},{5,6},{6,7},{8,9},{9,10},{10,11},{11... | collective-permute-start | bytes 786440 | tf_op jit(solution)/shard_map/ppermute | solution.py:100
  7.9 8.5 %collective-permute-start.2 = (f32[8,8192]{1,0:T(8,128)S(1)}, f32[8,8192]{1,0:T(8,128)S(1)}, u32[]{:S(2)}, u32[]{:S(2)}) collective-permute-start(f32[8,8192]{1,0:T(8,128)S(1)} %get-tuple-element.51), channel_id=1, source_target_pairs={{1,0},{2,1},{3,2},{4,3},{5,4},{6,5},{7,6},{9,8},{10,9},{11,10},{12... | collective-permute-start | bytes 786440 | tf_op jit(solution)/shard_map/ppermute | solution.py:101
  11.2 8.5 %collective-permute-start.1 = (f32[8,8192]{1,0:T(8,128)S(1)}, f32[8,8192]{1,0:T(8,128)S(1)}, u32[]{:S(2)}, u32[]{:S(2)}) collective-permute-start(f32[8,8192]{1,0:T(8,128)S(1)} %bitcast_add_fusion.5), channel_id=1, source_target_pairs={{0,1},{1,2},{8,9},{9,10},{16,17},{17,18},{24,25},{25,26},{32,33},{... | collective-permute-start | bytes 786440 | tf_op jit(solution)/shard_map/ppermute | solution.py:109
  16.5 8.1 %collective-permute-start.4 = (f32[8,8192]{1,0:T(8,128)S(1)}, f32[8,8192]{1,0:T(8,128)S(1)}, u32[]{:S(2)}, u32[]{:S(2)}) collective-permute-start(f32[8,8192]{1,0:T(8,128)S(1)} %bitcast_add_fusion.10), channel_id=1, source_target_pairs={{7,6},{6,5},{15,14},{14,13},{23,22},{22,21},{31,30},{30,29},{39,38... | collective-permute-start | bytes 786440 | tf_op jit(solution)/shard_map/ppermute | solution.py:112
  19.8 8.1 %collective-permute-start.3 = (f32[8,8192]{1,0:T(8,128)S(1)}, f32[8,8192]{1,0:T(8,128)S(1)}, u32[]{:S(2)}, u32[]{:S(2)}) collective-permute-start(f32[8,8192]{1,0:T(8,128)S(1)} %bitcast_add_fusion.6), channel_id=1, source_target_pairs={{0,1},{1,2},{2,3},{8,9},{9,10},{10,11},{16,17},{17,18},{18,19},{24... | collective-permute-start | bytes 786440 | tf_op jit(solution)/shard_map/ppermute | solution.py:109
  24.7 7.4 %collective-permute-start.6 = (f32[8,8192]{1,0:T(8,128)S(1)}, f32[8,8192]{1,0:T(8,128)S(1)}, u32[]{:S(2)}, u32[]{:S(2)}) collective-permute-start(f32[8,8192]{1,0:T(8,128)S(1)} %get-tuple-element.54), channel_id=1, source_target_pairs={{7,6},{6,5},{5,4},{15,14},{14,13},{13,12},{23,22},{22,21},{21,20},... | collective-permute-start | bytes 786440 | tf_op jit(solution)/shard_map/ppermute | solution.py:112
  28.0 7.4 %collective-permute-start.5 = (f32[8,8192]{1,0:T(8,128)S(1)}, f32[8,8192]{1,0:T(8,128)S(1)}, u32[]{:S(2)}, u32[]{:S(2)}) collective-permute-start(f32[8,8192]{1,0:T(8,128)S(1)} %bitcast_add_fusion.7), channel_id=1, source_target_pairs={{0,1},{1,2},{2,3},{3,4},{8,9},{9,10},{10,11},{11,12},{16,17},{17,1... | collective-permute-start | bytes 786440 | tf_op jit(solution)/shard_map/ppermute | solution.py:109
  32.1 29.4 %copy-start = (f32[4,8192]{1,0:T(4,128)S(1)}, f32[4,8192]{1,0:T(4,128)}, u32[]{:S(2)}) copy-start(f32[4,8192]{1,0:T(4,128)} %param.7) | copy-start | bytes 393220
  32.1 29.4 %copy-start.1 = (f32[4,8192]{1,0:T(4,128)S(1)}, f32[4,8192]{1,0:T(4,128)}, u32[]{:S(2)}) copy-start(f32[4,8192]{1,0:T(4,128)} %param.8) | copy-start | bytes 393220
  32.2 29.4 %copy-start.2 = (f32[4,8192]{1,0:T(4,128)S(1)}, f32[4,8192]{1,0:T(4,128)}, u32[]{:S(2)}) copy-start(f32[4,8192]{1,0:T(4,128)} %param.9) | copy-start | bytes 393220
  32.2 7.1 %collective-permute-start.8 = (f32[8,8192]{1,0:T(8,128)S(1)}, f32[8,8192]{1,0:T(8,128)S(1)}, u32[]{:S(2)}, u32[]{:S(2)}) collective-permute-start(f32[8,8192]{1,0:T(8,128)S(1)} %bitcast_add_fusion.1), channel_id=1, source_target_pairs={{7,6},{6,5},{5,4},{4,3},{15,14},{14,13},{13,12},{12,11},{23,22},{2... | collective-permute-start | bytes 786440 | tf_op jit(solution)/shard_map/ppermute | solution.py:112
  35.4 8.4 %collective-permute-start.7 = (f32[8,8192]{1,0:T(8,128)S(1)}, f32[8,8192]{1,0:T(8,128)S(1)}, u32[]{:S(2)}, u32[]{:S(2)}) collective-permute-start(f32[8,8192]{1,0:T(8,128)S(1)} %bitcast_add_fusion.8), channel_id=1, source_target_pairs={{0,1},{1,2},{2,3},{3,4},{4,5},{8,9},{9,10},{10,11},{11,12},{12,13}... | collective-permute-start | bytes 786440 | tf_op jit(solution)/shard_map/ppermute | solution.py:109
  39.3 8.7 %collective-permute-start.10 = (f32[8,8192]{1,0:T(8,128)S(1)}, f32[8,8192]{1,0:T(8,128)S(1)}, u32[]{:S(2)}, u32[]{:S(2)}) collective-permute-start(f32[8,8192]{1,0:T(8,128)S(1)} %bitcast_add_fusion), channel_id=1, source_target_pairs={{7,6},{6,5},{5,4},{4,3},{3,2},{15,14},{14,13},{13,12},{12,11},{11,... | collective-permute-start | bytes 786440 | tf_op jit(solution)/shard_map/ppermute | solution.py:112
  40.0 9.5 %collective-permute-start.12 = (f32[8,8192]{1,0:T(8,128)S(1)}, f32[8,8192]{1,0:T(8,128)S(1)}, u32[]{:S(2)}, u32[]{:S(2)}) collective-permute-start(f32[8,8192]{1,0:T(8,128)S(1)} %get-tuple-element.37), channel_id=1, source_target_pairs={{0,1},{7,6},{8,9},{15,14},{16,17},{23,22},{24,25},{31,30},{32,33},... | collective-permute-start | bytes 786440 | tf_op jit(solution)/shard_map/ppermute | solution.py:115
  43.8 17.6 %collective-permute-start.9 = (f32[8,8192]{1,0:T(8,128)S(1)}, f32[8,8192]{1,0:T(8,128)S(1)}, u32[]{:S(2)}, u32[]{:S(2)}) collective-permute-start(f32[8,8192]{1,0:T(8,128)S(1)} %bitcast_add_fusion.9), channel_id=1, source_target_pairs={{0,2},{1,3},{2,4},{3,5},{4,6},{5,7},{8,10},{9,11},{10,12},{11,13},... | collective-permute-start | bytes 786440 | tf_op jit(solution)/shard_map/ppermute | solution.py:118
  48.1 13.4 %collective-permute-start.11 = (f32[8,8192]{1,0:T(8,128)S(1)}, f32[8,8192]{1,0:T(8,128)S(1)}, u32[]{:S(2)}, u32[]{:S(2)}) collective-permute-start(f32[8,8192]{1,0:T(8,128)S(1)} %bitcast_add_fusion.4), channel_id=1, source_target_pairs={{2,0},{3,1},{4,2},{5,3},{6,4},{7,5},{10,8},{11,9},{12,10},{13,11},... | collective-permute-start | bytes 786440 | tf_op jit(solution)/shard_map/ppermute | solution.py:121
  83.5 13.9 %collective-permute-start.13 = (f32[2,4,128]{2,1,0:T(4,128)S(1)}, f32[2,4,128]{2,1,0:T(4,128)S(1)}, u32[]{:S(2)}, u32[]{:S(2)}) collective-permute-start(f32[2,4,128]{2,1,0:T(4,128)S(1)} %multiply_add_fusion.2), channel_id=1, source_target_pairs={{0,64},{64,0},{1,65},{65,1},{2,66},{66,2},{3,67},{67,3},{4,68},{68... | collective-permute-start | bytes 12296 | tf_op jit(solution)/shard_map/ppermute | solution.py:164

commit v6 on v5

--- a/solution.py
+++ b/solution.py
@@ -154,12 +154,13 @@
     far = lax.axis_index("far")
     sides = REPLICA_PARTS["far"]
     lines = REPLICA_PARTS["y"]
-    parts = weight.reshape(row_total, lines, sides, inner, LANES).transpose(1, 3, 2, 0, 4)
+    grid = (row_total, lines, sides, REPLICA_PARTS["x"], REPLICA_PARTS["core"], LANES)
+    parts = weight.reshape(grid).transpose((3, 1, 4, 2, 0, 5))
     parts = parts.reshape((lines * inner, sides) + still.shape)
     mine = lax.broadcasted_iota(jnp.int32, parts.shape[1:], 0) == far
     added = jnp.where(mine, still[None], 0.0)
     parts, added, still, far = lax.optimization_barrier((parts, added, still, far))
-    parts = lax.all_to_all(parts, ("y", "x", "core"), 0, 0, tiled=True)
+    parts = lax.all_to_all(parts, ("x", "y", "core"), 0, 0, tiled=True)
     share = jnp.sum(parts, axis=0) * (pull / replicas) + added
     known = share + lax.ppermute(share, "far", [(0, 1), (1, 0)])
     new_global = pick(known, far)
@@ -168,9 +169,9 @@
     sent, new_global, new_momentum = lax.optimization_barrier(
         (copies(known, lines * inner), new_global, new_momentum)
     )
-    gathered = lax.all_to_all(sent, ("y", "x", "core"), 0, 0, tiled=True)
-    gathered = gathered.reshape((lines, inner, sides) + still.shape)
-    gathered = gathered.transpose(3, 0, 2, 1, 4).reshape(row_total, columns)
+    gathered = lax.all_to_all(sent, ("x", "y", "core"), 0, 0, tiled=True)
+    gathered = gathered.reshape(tuple(grid[k] for k in (3, 1, 4, 2, 0, 5)))
+    gathered = gathered.transpose((4, 1, 3, 0, 2, 5)).reshape(row_total, columns)
     new_local = mix_share * weight + (1.0 - mix_share) * gathered
     return (new_local, first_moment, second_moment, new_global, new_momentum)
 

time: 111 us -> 112 us (level)
  no operation moved by 1% of the time
where the time goes in v6:
time: 112 us; the launch traced here: 111 us
  starting transfers between devices  48.7 us (43%)
  blocking collectives  32.9 us (29%)
  waiting for transfers between devices  22.4 us (20%)
  other arithmetic  2.93 us (3%)
  Pallas kernels  2.76 us (2%)
    all_to_all x1, blocking collectives, body(): parts = lax.all_to_all(parts, ('x', 'y', 'core'), 0, 0, tiled=True)  20.7 us
    ppermute x4, starting transfers between devices, reduce_line(): up = lax.ppermute(up_sent, 'dp', [(k, k + 1) for k in range(step)])  18 us
    ppermute x1, starting transfers between devices, body(): known = share + lax.ppermute(share, 'far', [(0, 1), (1, 0)])  12.9 us
    all_to_all x1, blocking collectives, body(): gathered = lax.all_to_all(sent, ('x', 'y', 'core'), 0, 0, tiled=True)  12.1 us
    ppermute x1, waiting for transfers between devices, reduce_line(): down = lax.ppermute(down_sent, 'dp', [(k + 2, k) for k in range(last)])  12 us
    ppermute x4, waiting for transfers between devices, reduce_line(): up = lax.ppermute(up_sent, 'dp', [(k, k + 1) for k in range(step)])  7.44 us
    ppermute x1, starting transfers between devices, reduce_line(): up = lax.ppermute(up_sent, 'dp', rights)  4.39 us
    ppermute x1, starting transfers between devices, reduce_line(): up = lax.ppermute(up_sent, 'dp', [(k, k + 2) for k in range(last)])  4.16 us
  transfers between devices with their start and end apart: 14, of which 6 were waited for; matrix products, arithmetic and copies ran while one was open for 0% of the time, Pallas kernels for 0%

profile of v6, /device:TPU:1, one launch (start us, length us, event | category | flops | bytes accessed | tf_op | source)
XLA Modules:
  0.0 111.3 jit_solution(15435417444194102236)
XLA Ops:
  0.7 2.8 %partial_gradients.1 = f32[8,8,8192]{2,1,0:T(8,128)S(1)} custom-call(bf16[2,32,128]{2,1,0:T(8,128)(2,1)} %hidden_hbm.1, bf16[2,128,8192]{2,1,0:T(8,128)(2,1)} %grads_hbm.1), custom_call_target="tpu_custom_call" | custom-call | tf_op jit(solution)/shard_map/partial_gradients/pallas_call | solution.py:71
  3.5 0.1 dynamic-slice_bitcast_fusion
  3.5 4.4 %collective-permute-start = (f32[8,8192]{1,0:T(8,128)S(1)}, f32[8,8192]{1,0:T(8,128)S(1)}, u32[]{:S(2)}, u32[]{:S(2)}) collective-permute-start(f32[8,8192]{1,0:T(8,128)S(1)} %get-tuple-element.52), channel_id=1, source_target_pairs={{0,1},{1,2},{2,3},{3,4},{4,5},{5,6},{6,7},{8,9},{9,10},{10,11},{11... | collective-permute-start | bytes 786440 | tf_op jit(solution)/shard_map/ppermute | solution.py:100
  7.9 1.3 %collective-permute-start.2 = (f32[8,8192]{1,0:T(8,128)S(1)}, f32[8,8192]{1,0:T(8,128)S(1)}, u32[]{:S(2)}, u32[]{:S(2)}) collective-permute-start(f32[8,8192]{1,0:T(8,128)S(1)} %get-tuple-element.51), channel_id=1, source_target_pairs={{1,0},{2,1},{3,2},{4,3},{5,4},{6,5},{7,6},{9,8},{10,9},{11,10},{12... | collective-permute-start | bytes 786440 | tf_op jit(solution)/shard_map/ppermute | solution.py:101
  9.3 1.9 %collective-permute-done = f32[8,8192]{1,0:T(8,128)S(1)} collective-permute-done((f32[8,8192]{1,0:T(8,128)S(1)}, f32[8,8192]{1,0:T(8,128)S(1)}, u32[]{:S(2)}, u32[]{:S(2)}) %collective-permute-start) | collective-permute-done | bytes 262176 | tf_op jit(solution)/shard_map/ppermute | solution.py:100
  11.2 5.2 %collective-permute-start.1 = (f32[8,8192]{1,0:T(8,128)S(1)}, f32[8,8192]{1,0:T(8,128)S(1)}, u32[]{:S(2)}, u32[]{:S(2)}) collective-permute-start(f32[8,8192]{1,0:T(8,128)S(1)} %bitcast_add_fusion.5), channel_id=1, source_target_pairs={{0,1},{1,2},{8,9},{9,10},{16,17},{17,18},{24,25},{25,26},{32,33},{... | collective-permute-start | bytes 786440 | tf_op jit(solution)/shard_map/ppermute | solution.py:109
  16.5 0.7 collective-permute-start.4
  17.2 2.5 %collective-permute-done.1 = f32[8,8192]{1,0:T(8,128)S(1)} collective-permute-done((f32[8,8192]{1,0:T(8,128)S(1)}, f32[8,8192]{1,0:T(8,128)S(1)}, u32[]{:S(2)}, u32[]{:S(2)}) %collective-permute-start.1) | collective-permute-done | bytes 262176 | tf_op jit(solution)/shard_map/ppermute | solution.py:109
  19.8 4.9 %collective-permute-start.3 = (f32[8,8192]{1,0:T(8,128)S(1)}, f32[8,8192]{1,0:T(8,128)S(1)}, u32[]{:S(2)}, u32[]{:S(2)}) collective-permute-start(f32[8,8192]{1,0:T(8,128)S(1)} %bitcast_add_fusion.6), channel_id=1, source_target_pairs={{0,1},{1,2},{2,3},{8,9},{9,10},{10,11},{16,17},{17,18},{18,19},{24... | collective-permute-start | bytes 786440 | tf_op jit(solution)/shard_map/ppermute | solution.py:109
  24.6 0.1 bitcast_add_fusion.2
  24.7 0.7 collective-permute-start.6
  25.4 2.5 %collective-permute-done.3 = f32[8,8192]{1,0:T(8,128)S(1)} collective-permute-done((f32[8,8192]{1,0:T(8,128)S(1)}, f32[8,8192]{1,0:T(8,128)S(1)}, u32[]{:S(2)}, u32[]{:S(2)}) %collective-permute-start.3) | collective-permute-done | bytes 262176 | tf_op jit(solution)/shard_map/ppermute | solution.py:109
  28.0 4.1 %collective-permute-start.5 = (f32[8,8192]{1,0:T(8,128)S(1)}, f32[8,8192]{1,0:T(8,128)S(1)}, u32[]{:S(2)}, u32[]{:S(2)}) collective-permute-start(f32[8,8192]{1,0:T(8,128)S(1)} %bitcast_add_fusion.7), channel_id=1, source_target_pairs={{0,1},{1,2},{2,3},{3,4},{8,9},{9,10},{10,11},{11,12},{16,17},{17,1... | collective-permute-start | bytes 786440 | tf_op jit(solution)/shard_map/ppermute | solution.py:109
  32.2 0.8 collective-permute-start.8
  33.0 2.4 %collective-permute-done.5 = f32[8,8192]{1,0:T(8,128)S(1)} collective-permute-done((f32[8,8192]{1,0:T(8,128)S(1)}, f32[8,8192]{1,0:T(8,128)S(1)}, u32[]{:S(2)}, u32[]{:S(2)}) %collective-permute-start.5) | collective-permute-done | bytes 262176 | tf_op jit(solution)/shard_map/ppermute | solution.py:109
  35.4 3.8 %collective-permute-start.7 = (f32[8,8192]{1,0:T(8,128)S(1)}, f32[8,8192]{1,0:T(8,128)S(1)}, u32[]{:S(2)}, u32[]{:S(2)}) collective-permute-start(f32[8,8192]{1,0:T(8,128)S(1)} %bitcast_add_fusion.8), channel_id=1, source_target_pairs={{0,1},{1,2},{2,3},{3,4},{4,5},{8,9},{9,10},{10,11},{11,12},{12,13}... | collective-permute-start | bytes 786440 | tf_op jit(solution)/shard_map/ppermute | solution.py:109
  39.3 0.7 collective-permute-start.10
  40.0 3.8 %collective-permute-start.12 = (f32[8,8192]{1,0:T(8,128)S(1)}, f32[8,8192]{1,0:T(8,128)S(1)}, u32[]{:S(2)}, u32[]{:S(2)}) collective-permute-start(f32[8,8192]{1,0:T(8,128)S(1)} %get-tuple-element.37), channel_id=1, source_target_pairs={{0,1},{7,6},{8,9},{15,14},{16,17},{23,22},{24,25},{31,30},{32,33},... | collective-permute-start | bytes 786440 | tf_op jit(solution)/shard_map/ppermute | solution.py:115
  43.8 4.2 %collective-permute-start.9 = (f32[8,8192]{1,0:T(8,128)S(1)}, f32[8,8192]{1,0:T(8,128)S(1)}, u32[]{:S(2)}, u32[]{:S(2)}) collective-permute-start(f32[8,8192]{1,0:T(8,128)S(1)} %bitcast_add_fusion.9), channel_id=1, source_target_pairs={{0,2},{1,3},{2,4},{3,5},{4,6},{5,7},{8,10},{9,11},{10,12},{11,13},... | collective-permute-start | bytes 786440 | tf_op jit(solution)/shard_map/ppermute | solution.py:118
  48.1 1.3 %collective-permute-start.11 = (f32[8,8192]{1,0:T(8,128)S(1)}, f32[8,8192]{1,0:T(8,128)S(1)}, u32[]{:S(2)}, u32[]{:S(2)}) collective-permute-start(f32[8,8192]{1,0:T(8,128)S(1)} %bitcast_add_fusion.4), channel_id=1, source_target_pairs={{2,0},{3,1},{4,2},{5,3},{6,4},{7,5},{10,8},{11,9},{12,10},{13,11},... | collective-permute-start | bytes 786440 | tf_op jit(solution)/shard_map/ppermute | solution.py:121
  49.4 0.1 broadcast_select_fusion
  49.4 12.0 %collective-permute-done.11 = f32[8,8192]{1,0:T(8,128)S(1)} collective-permute-done((f32[8,8192]{1,0:T(8,128)S(1)}, f32[8,8192]{1,0:T(8,128)S(1)}, u32[]{:S(2)}, u32[]{:S(2)}) %collective-permute-start.11) | collective-permute-done | bytes 262176 | tf_op jit(solution)/shard_map/ppermute | solution.py:121
  61.6 1.1 multiply_subtract_fusion
  62.7 0.1 reshape.24
  62.9 0.1 copy.16
  62.9 20.7 %all_to_all.10 = f32[32,2,4,128]{3,2,1,0:T(4,128)S(1)} all-to-all(f32[32,2,4,128]{3,2,1,0:T(4,128)S(1)} %copy.16), channel_id=1, replica_groups=mesh['y'=4,'far'=2,'x'=4,'core'=2,'dp'=8] {'x','y','core'}, dimensions={0} | all-to-all | bytes 262144 | tf_op jit(solution)/shard_map/all_to_all | solution.py:163
  83.7 12.9 %collective-permute-start.13 = (f32[2,4,128]{2,1,0:T(4,128)S(1)}, f32[2,4,128]{2,1,0:T(4,128)S(1)}, u32[]{:S(2)}, u32[]{:S(2)}) collective-permute-start(f32[2,4,128]{2,1,0:T(4,128)S(1)} %multiply_add_fusion.2), channel_id=1, source_target_pairs={{0,64},{64,0},{1,65},{65,1},{2,66},{66,2},{3,67},{67,3},{4,68},{68... | collective-permute-start | bytes 12296 | tf_op jit(solution)/shard_map/ppermute | solution.py:165
  96.6 1.0 collective-permute-done.13
  97.6 0.6 subtract_add_fusion
  98.2 12.1 %all_to_all.11 = f32[32,2,4,128]{3,2,1,0:T(4,128)S(1)} all-to-all(f32[32,2,4,128]{3,2,1,0:T(4,128)S(1)} %broadcast_in_dim.27), channel_id=1, replica_groups=mesh['y'=4,'far'=2,'x'=4,'core'=2,'dp'=8] {'x','y','core'}, dimensions={0} | all-to-all | bytes 262144 | tf_op jit(solution)/shard_map/all_to_all | solution.py:172
  110.5 0.1 reshape.27
  110.6 0.7 add_multiply_fusion
  (37 shorter events, 0.6 us)
Async XLA Ops:
  0.7 8.6 %copy-start.3 = (f32[4,128]{1,0:T(4,128)S(1)}, f32[4,128]{1,0:T(4,128)}, u32[]{:S(2)}) copy-start(f32[4,128]{1,0:T(4,128)} %param.12) | copy-start | bytes 6148
  0.7 8.6 %copy-start.4 = (f32[4,128]{1,0:T(4,128)S(1)}, f32[4,128]{1,0:T(4,128)}, u32[]{:S(2)}) copy-start(f32[4,128]{1,0:T(4,128)} %param.13) | copy-start | bytes 6148
  3.5 7.7 %collective-permute-start = (f32[8,8192]{1,0:T(8,128)S(1)}, f32[8,8192]{1,0:T(8,128)S(1)}, u32[]{:S(2)}, u32[]{:S(2)}) collective-permute-start(f32[8,8192]{1,0:T(8,128)S(1)} %get-tuple-element.52), channel_id=1, source_target_pairs={{0,1},{1,2},{2,3},{3,4},{4,5},{5,6},{6,7},{8,9},{9,10},{10,11},{11... | collective-permute-start | bytes 786440 | tf_op jit(solution)/shard_map/ppermute | solution.py:100
  7.9 8.5 %collective-permute-start.2 = (f32[8,8192]{1,0:T(8,128)S(1)}, f32[8,8192]{1,0:T(8,128)S(1)}, u32[]{:S(2)}, u32[]{:S(2)}) collective-permute-start(f32[8,8192]{1,0:T(8,128)S(1)} %get-tuple-element.51), channel_id=1, source_target_pairs={{1,0},{2,1},{3,2},{4,3},{5,4},{6,5},{7,6},{9,8},{10,9},{11,10},{12... | collective-permute-start | bytes 786440 | tf_op jit(solution)/shard_map/ppermute | solution.py:101
  11.2 8.5 %collective-permute-start.1 = (f32[8,8192]{1,0:T(8,128)S(1)}, f32[8,8192]{1,0:T(8,128)S(1)}, u32[]{:S(2)}, u32[]{:S(2)}) collective-permute-start(f32[8,8192]{1,0:T(8,128)S(1)} %bitcast_add_fusion.5), channel_id=1, source_target_pairs={{0,1},{1,2},{8,9},{9,10},{16,17},{17,18},{24,25},{25,26},{32,33},{... | collective-permute-start | bytes 786440 | tf_op jit(solution)/shard_map/ppermute | solution.py:109
  16.5 8.1 %collective-permute-start.4 = (f32[8,8192]{1,0:T(8,128)S(1)}, f32[8,8192]{1,0:T(8,128)S(1)}, u32[]{:S(2)}, u32[]{:S(2)}) collective-permute-start(f32[8,8192]{1,0:T(8,128)S(1)} %bitcast_add_fusion.10), channel_id=1, source_target_pairs={{7,6},{6,5},{15,14},{14,13},{23,22},{22,21},{31,30},{30,29},{39,38... | collective-permute-start | bytes 786440 | tf_op jit(solution)/shard_map/ppermute | solution.py:112
  19.8 8.1 %collective-permute-start.3 = (f32[8,8192]{1,0:T(8,128)S(1)}, f32[8,8192]{1,0:T(8,128)S(1)}, u32[]{:S(2)}, u32[]{:S(2)}) collective-permute-start(f32[8,8192]{1,0:T(8,128)S(1)} %bitcast_add_fusion.6), channel_id=1, source_target_pairs={{0,1},{1,2},{2,3},{8,9},{9,10},{10,11},{16,17},{17,18},{18,19},{24... | collective-permute-start | bytes 786440 | tf_op jit(solution)/shard_map/ppermute | solution.py:109
  24.7 7.4 %collective-permute-start.6 = (f32[8,8192]{1,0:T(8,128)S(1)}, f32[8,8192]{1,0:T(8,128)S(1)}, u32[]{:S(2)}, u32[]{:S(2)}) collective-permute-start(f32[8,8192]{1,0:T(8,128)S(1)} %get-tuple-element.54), channel_id=1, source_target_pairs={{7,6},{6,5},{5,4},{15,14},{14,13},{13,12},{23,22},{22,21},{21,20},... | collective-permute-start | bytes 786440 | tf_op jit(solution)/shard_map/ppermute | solution.py:112
  28.0 7.4 %collective-permute-start.5 = (f32[8,8192]{1,0:T(8,128)S(1)}, f32[8,8192]{1,0:T(8,128)S(1)}, u32[]{:S(2)}, u32[]{:S(2)}) collective-permute-start(f32[8,8192]{1,0:T(8,128)S(1)} %bitcast_add_fusion.7), channel_id=1, source_target_pairs={{0,1},{1,2},{2,3},{3,4},{8,9},{9,10},{10,11},{11,12},{16,17},{17,1... | collective-permute-start | bytes 786440 | tf_op jit(solution)/shard_map/ppermute | solution.py:109
  32.1 29.4 %copy-start = (f32[4,8192]{1,0:T(4,128)S(1)}, f32[4,8192]{1,0:T(4,128)}, u32[]{:S(2)}) copy-start(f32[4,8192]{1,0:T(4,128)} %param.7) | copy-start | bytes 393220
  32.1 29.4 %copy-start.1 = (f32[4,8192]{1,0:T(4,128)S(1)}, f32[4,8192]{1,0:T(4,128)}, u32[]{:S(2)}) copy-start(f32[4,8192]{1,0:T(4,128)} %param.8) | copy-start | bytes 393220
  32.2 29.4 %copy-start.2 = (f32[4,8192]{1,0:T(4,128)S(1)}, f32[4,8192]{1,0:T(4,128)}, u32[]{:S(2)}) copy-start(f32[4,8192]{1,0:T(4,128)} %param.9) | copy-start | bytes 393220
  32.2 7.1 %collective-permute-start.8 = (f32[8,8192]{1,0:T(8,128)S(1)}, f32[8,8192]{1,0:T(8,128)S(1)}, u32[]{:S(2)}, u32[]{:S(2)}) collective-permute-start(f32[8,8192]{1,0:T(8,128)S(1)} %bitcast_add_fusion.1), channel_id=1, source_target_pairs={{7,6},{6,5},{5,4},{4,3},{15,14},{14,13},{13,12},{12,11},{23,22},{2... | collective-permute-start | bytes 786440 | tf_op jit(solution)/shard_map/ppermute | solution.py:112
  35.4 8.4 %collective-permute-start.7 = (f32[8,8192]{1,0:T(8,128)S(1)}, f32[8,8192]{1,0:T(8,128)S(1)}, u32[]{:S(2)}, u32[]{:S(2)}) collective-permute-start(f32[8,8192]{1,0:T(8,128)S(1)} %bitcast_add_fusion.8), channel_id=1, source_target_pairs={{0,1},{1,2},{2,3},{3,4},{4,5},{8,9},{9,10},{10,11},{11,12},{12,13}... | collective-permute-start | bytes 786440 | tf_op jit(solution)/shard_map/ppermute | solution.py:109
  39.3 8.7 %collective-permute-start.10 = (f32[8,8192]{1,0:T(8,128)S(1)}, f32[8,8192]{1,0:T(8,128)S(1)}, u32[]{:S(2)}, u32[]{:S(2)}) collective-permute-start(f32[8,8192]{1,0:T(8,128)S(1)} %bitcast_add_fusion), channel_id=1, source_target_pairs={{7,6},{6,5},{5,4},{4,3},{3,2},{15,14},{14,13},{13,12},{12,11},{11,... | collective-permute-start | bytes 786440 | tf_op jit(solution)/shard_map/ppermute | solution.py:112
  40.0 9.5 %collective-permute-start.12 = (f32[8,8192]{1,0:T(8,128)S(1)}, f32[8,8192]{1,0:T(8,128)S(1)}, u32[]{:S(2)}, u32[]{:S(2)}) collective-permute-start(f32[8,8192]{1,0:T(8,128)S(1)} %get-tuple-element.37), channel_id=1, source_target_pairs={{0,1},{7,6},{8,9},{15,14},{16,17},{23,22},{24,25},{31,30},{32,33},... | collective-permute-start | bytes 786440 | tf_op jit(solution)/shard_map/ppermute | solution.py:115
  43.8 17.6 %collective-permute-start.9 = (f32[8,8192]{1,0:T(8,128)S(1)}, f32[8,8192]{1,0:T(8,128)S(1)}, u32[]{:S(2)}, u32[]{:S(2)}) collective-permute-start(f32[8,8192]{1,0:T(8,128)S(1)} %bitcast_add_fusion.9), channel_id=1, source_target_pairs={{0,2},{1,3},{2,4},{3,5},{4,6},{5,7},{8,10},{9,11},{10,12},{11,13},... | collective-permute-start | bytes 786440 | tf_op jit(solution)/shard_map/ppermute | solution.py:118
  48.1 13.4 %collective-permute-start.11 = (f32[8,8192]{1,0:T(8,128)S(1)}, f32[8,8192]{1,0:T(8,128)S(1)}, u32[]{:S(2)}, u32[]{:S(2)}) collective-permute-start(f32[8,8192]{1,0:T(8,128)S(1)} %bitcast_add_fusion.4), channel_id=1, source_target_pairs={{2,0},{3,1},{4,2},{5,3},{6,4},{7,5},{10,8},{11,9},{12,10},{13,11},... | collective-permute-start | bytes 786440 | tf_op jit(solution)/shard_map/ppermute | solution.py:121
  83.7 13.9 %collective-permute-start.13 = (f32[2,4,128]{2,1,0:T(4,128)S(1)}, f32[2,4,128]{2,1,0:T(4,128)S(1)}, u32[]{:S(2)}, u32[]{:S(2)}) collective-permute-start(f32[2,4,128]{2,1,0:T(4,128)S(1)} %multiply_add_fusion.2), channel_id=1, source_target_pairs={{0,64},{64,0},{1,65},{65,1},{2,66},{66,2},{3,67},{67,3},{4,68},{68... | collective-permute-start | bytes 12296 | tf_op jit(solution)/shard_map/ppermute | solution.py:165

commit v7 on v5

--- a/solution.py
+++ b/solution.py
@@ -110,15 +110,15 @@
         down, _ = lax.optimization_barrier((down, up_sent))
         down_sent = at(step) + down
         down = lax.ppermute(down_sent, "dp", [(end - k, end - k - 1) for k in range(step)])
-        if step == 5:
-            edge, _ = lax.optimization_barrier((at(jnp.where(place == 0, 1, -1)), down_sent))
-            edge = lax.ppermute(edge, "dp", [(0, 1), (end, end - 1)])
     up, _ = lax.optimization_barrier((up, down_sent))
     up_sent = at(2) + up
     up = lax.ppermute(up_sent, "dp", [(k, k + 2) for k in range(last)])
     down, _ = lax.optimization_barrier((down, up_sent))
     down_sent = at(-2) + down
     down = lax.ppermute(down_sent, "dp", [(k + 2, k) for k in range(last)])
+    edge = at(jnp.where(place == 0, 1, -1))
+    edge, _ = lax.optimization_barrier((edge, down_sent))
+    edge = lax.ppermute(edge, "dp", [(0, 1), (end, end - 1)])
     return (up + down) + (own + edge)
 
 

time: 111 us -> 112 us (level)
  starting transfers between devices: 48.7 us -> 51.7 us
  waiting for transfers between devices: 22.4 us -> 19.7 us
    ppermute x1, waiting for transfers between devices: 12 us -> 1.82 us  [reduce_line(): down = lax.ppermute(down_sent, 'dp', [(k + 2, k) for k in range(last)])]
    ppermute x1, waiting for transfers between devices: 0.01 us -> 4.61 us  [reduce_line(): edge = lax.ppermute(edge, 'dp', [(0, 1), (end, end - 1)])]
    ppermute x4, waiting for transfers between devices: 7.44 us -> 10.4 us  [reduce_line(): up = lax.ppermute(up_sent, 'dp', [(k, k + 1) for k in range(step)])]
    ppermute x1, starting transfers between devices: 12.9 us -> 15.1 us  [body(): known = share + lax.ppermute(share, 'far', [(0, 1), (1, 0)])]
  transfers between devices with their start and end apart: 14 -> 14, of which waited for: 6 -> 8; matrix products, arithmetic and copies ran while one was open for 0% -> 0% of each run, Pallas kernels for 0% -> 0%
where the time goes in v7:
time: 112 us; the launch traced here: 111 us
  starting transfers between devices  51.7 us (46%)
  blocking collectives  32.9 us (29%)
  waiting for transfers between devices  19.7 us (18%)
  other arithmetic  2.99 us (3%)
  Pallas kernels  2.76 us (2%)
    all_to_all x1, blocking collectives, body(): parts = lax.all_to_all(parts, ('y', 'x', 'core'), 0, 0, tiled=True)  20.8 us
    ppermute x4, starting transfers between devices, reduce_line(): up = lax.ppermute(up_sent, 'dp', [(k, k + 1) for k in range(step)])  18 us
    ppermute x1, starting transfers between devices, body(): known = share + lax.ppermute(share, 'far', [(0, 1), (1, 0)])  15.1 us
    all_to_all x1, blocking collectives, body(): gathered = lax.all_to_all(sent, ('y', 'x', 'core'), 0, 0, tiled=True)  12.1 us
    ppermute x4, waiting for transfers between devices, reduce_line(): up = lax.ppermute(up_sent, 'dp', [(k, k + 1) for k in range(step)])  10.4 us
    ppermute x1, starting transfers between devices, reduce_line(): up = lax.ppermute(up_sent, 'dp', [(k, k + 2) for k in range(last)])  5.07 us
    ppermute x1, waiting for transfers between devices, reduce_line(): edge = lax.ppermute(edge, 'dp', [(0, 1), (end, end - 1)])  4.61 us
    ppermute x1, starting transfers between devices, reduce_line(): up = lax.ppermute(up_sent, 'dp', rights)  4.39 us
  transfers between devices with their start and end apart: 14, of which 8 were waited for; matrix products, arithmetic and copies ran while one was open for 0% of the time, Pallas kernels for 0%

profile of v7, /device:TPU:1, one launch (start us, length us, event | category | flops | bytes accessed | tf_op | source)
XLA Modules:
  0.0 111.3 jit_solution(7248798248266632154)
XLA Ops:
  0.7 2.8 %partial_gradients.1 = f32[8,8,8192]{2,1,0:T(8,128)S(1)} custom-call(bf16[2,32,128]{2,1,0:T(8,128)(2,1)} %hidden_hbm.1, bf16[2,128,8192]{2,1,0:T(8,128)(2,1)} %grads_hbm.1), custom_call_target="tpu_custom_call" | custom-call | tf_op jit(solution)/shard_map/partial_gradients/pallas_call | solution.py:71
  3.5 4.4 %collective-permute-start = (f32[8,8192]{1,0:T(8,128)S(1)}, f32[8,8192]{1,0:T(8,128)S(1)}, u32[]{:S(2)}, u32[]{:S(2)}) collective-permute-start(f32[8,8192]{1,0:T(8,128)S(1)} %get-tuple-element.52), channel_id=1, source_target_pairs={{0,1},{1,2},{2,3},{3,4},{4,5},{5,6},{6,7},{8,9},{9,10},{10,11},{11... | collective-permute-start | bytes 786440 | tf_op jit(solution)/shard_map/ppermute | solution.py:100
  7.9 1.3 %collective-permute-start.2 = (f32[8,8192]{1,0:T(8,128)S(1)}, f32[8,8192]{1,0:T(8,128)S(1)}, u32[]{:S(2)}, u32[]{:S(2)}) collective-permute-start(f32[8,8192]{1,0:T(8,128)S(1)} %get-tuple-element.51), channel_id=1, source_target_pairs={{1,0},{2,1},{3,2},{4,3},{5,4},{6,5},{7,6},{9,8},{10,9},{11,10},{12... | collective-permute-start | bytes 786440 | tf_op jit(solution)/shard_map/ppermute | solution.py:101
  9.3 1.9 %collective-permute-done = f32[8,8192]{1,0:T(8,128)S(1)} collective-permute-done((f32[8,8192]{1,0:T(8,128)S(1)}, f32[8,8192]{1,0:T(8,128)S(1)}, u32[]{:S(2)}, u32[]{:S(2)}) %collective-permute-start) | collective-permute-done | bytes 262176 | tf_op jit(solution)/shard_map/ppermute | solution.py:100
  11.2 5.2 %collective-permute-start.1 = (f32[8,8192]{1,0:T(8,128)S(1)}, f32[8,8192]{1,0:T(8,128)S(1)}, u32[]{:S(2)}, u32[]{:S(2)}) collective-permute-start(f32[8,8192]{1,0:T(8,128)S(1)} %bitcast_add_fusion.5), channel_id=1, source_target_pairs={{0,1},{1,2},{8,9},{9,10},{16,17},{17,18},{24,25},{25,26},{32,33},{... | collective-permute-start | bytes 786440 | tf_op jit(solution)/shard_map/ppermute | solution.py:109
  16.5 0.7 collective-permute-start.4
  17.2 2.5 %collective-permute-done.1 = f32[8,8192]{1,0:T(8,128)S(1)} collective-permute-done((f32[8,8192]{1,0:T(8,128)S(1)}, f32[8,8192]{1,0:T(8,128)S(1)}, u32[]{:S(2)}, u32[]{:S(2)}) %collective-permute-start.1) | collective-permute-done | bytes 262176 | tf_op jit(solution)/shard_map/ppermute | solution.py:109
  19.8 4.9 %collective-permute-start.3 = (f32[8,8192]{1,0:T(8,128)S(1)}, f32[8,8192]{1,0:T(8,128)S(1)}, u32[]{:S(2)}, u32[]{:S(2)}) collective-permute-start(f32[8,8192]{1,0:T(8,128)S(1)} %bitcast_add_fusion.6), channel_id=1, source_target_pairs={{0,1},{1,2},{2,3},{8,9},{9,10},{10,11},{16,17},{17,18},{18,19},{24... | collective-permute-start | bytes 786440 | tf_op jit(solution)/shard_map/ppermute | solution.py:109
  24.6 0.1 bitcast_add_fusion.2
  24.7 0.7 collective-permute-start.6
  25.4 2.5 %collective-permute-done.3 = f32[8,8192]{1,0:T(8,128)S(1)} collective-permute-done((f32[8,8192]{1,0:T(8,128)S(1)}, f32[8,8192]{1,0:T(8,128)S(1)}, u32[]{:S(2)}, u32[]{:S(2)}) %collective-permute-start.3) | collective-permute-done | bytes 262176 | tf_op jit(solution)/shard_map/ppermute | solution.py:109
  28.0 4.1 %collective-permute-start.5 = (f32[8,8192]{1,0:T(8,128)S(1)}, f32[8,8192]{1,0:T(8,128)S(1)}, u32[]{:S(2)}, u32[]{:S(2)}) collective-permute-start(f32[8,8192]{1,0:T(8,128)S(1)} %bitcast_add_fusion.7), channel_id=1, source_target_pairs={{0,1},{1,2},{2,3},{3,4},{8,9},{9,10},{10,11},{11,12},{16,17},{17,1... | collective-permute-start | bytes 786440 | tf_op jit(solution)/shard_map/ppermute | solution.py:109
  32.2 0.8 collective-permute-start.8
  33.0 2.4 %collective-permute-done.5 = f32[8,8192]{1,0:T(8,128)S(1)} collective-permute-done((f32[8,8192]{1,0:T(8,128)S(1)}, f32[8,8192]{1,0:T(8,128)S(1)}, u32[]{:S(2)}, u32[]{:S(2)}) %collective-permute-start.5) | collective-permute-done | bytes 262176 | tf_op jit(solution)/shard_map/ppermute | solution.py:109
  35.4 3.8 %collective-permute-start.7 = (f32[8,8192]{1,0:T(8,128)S(1)}, f32[8,8192]{1,0:T(8,128)S(1)}, u32[]{:S(2)}, u32[]{:S(2)}) collective-permute-start(f32[8,8192]{1,0:T(8,128)S(1)} %bitcast_add_fusion.8), channel_id=1, source_target_pairs={{0,1},{1,2},{2,3},{3,4},{4,5},{8,9},{9,10},{10,11},{11,12},{12,13}... | collective-permute-start | bytes 786440 | tf_op jit(solution)/shard_map/ppermute | solution.py:109
  39.3 0.7 collective-permute-start.10
  40.0 2.9 %collective-permute-done.7 = f32[8,8192]{1,0:T(8,128)S(1)} collective-permute-done((f32[8,8192]{1,0:T(8,128)S(1)}, f32[8,8192]{1,0:T(8,128)S(1)}, u32[]{:S(2)}, u32[]{:S(2)}) %collective-permute-start.7) | collective-permute-done | bytes 262176 | tf_op jit(solution)/shard_map/ppermute | solution.py:109
  42.9 5.1 %collective-permute-start.9 = (f32[8,8192]{1,0:T(8,128)S(1)}, f32[8,8192]{1,0:T(8,128)S(1)}, u32[]{:S(2)}, u32[]{:S(2)}) collective-permute-start(f32[8,8192]{1,0:T(8,128)S(1)} %bitcast_add_fusion.9), channel_id=1, source_target_pairs={{0,2},{1,3},{2,4},{3,5},{4,6},{5,7},{8,10},{9,11},{10,12},{11,13},... | collective-permute-start | bytes 786440 | tf_op jit(solution)/shard_map/ppermute | solution.py:115
  48.1 1.3 %collective-permute-start.11 = (f32[8,8192]{1,0:T(8,128)S(1)}, f32[8,8192]{1,0:T(8,128)S(1)}, u32[]{:S(2)}, u32[]{:S(2)}) collective-permute-start(f32[8,8192]{1,0:T(8,128)S(1)} %bitcast_add_fusion.4), channel_id=1, source_target_pairs={{2,0},{3,1},{4,2},{5,3},{6,4},{7,5},{10,8},{11,9},{12,10},{13,11},... | collective-permute-start | bytes 786440 | tf_op jit(solution)/shard_map/ppermute | solution.py:118
  49.4 3.7 %collective-permute-start.12 = (f32[8,8192]{1,0:T(8,128)S(1)}, f32[8,8192]{1,0:T(8,128)S(1)}, u32[]{:S(2)}, u32[]{:S(2)}) collective-permute-start(f32[8,8192]{1,0:T(8,128)S(1)} %get-tuple-element.37), channel_id=1, source_target_pairs={{0,1},{7,6},{8,9},{15,14},{16,17},{23,22},{24,25},{31,30},{32,33},... | collective-permute-start | bytes 786440 | tf_op jit(solution)/shard_map/ppermute | solution.py:121
  53.0 0.1 broadcast_select_fusion
  53.1 4.6 %collective-permute-done.12 = f32[8,8192]{1,0:T(8,128)S(1)} collective-permute-done((f32[8,8192]{1,0:T(8,128)S(1)}, f32[8,8192]{1,0:T(8,128)S(1)}, u32[]{:S(2)}, u32[]{:S(2)}) %collective-permute-start.12) | collective-permute-done | bytes 262176 | tf_op jit(solution)/shard_map/ppermute | solution.py:121
  57.7 1.8 %collective-permute-done.11 = f32[8,8192]{1,0:T(8,128)S(1)} collective-permute-done((f32[8,8192]{1,0:T(8,128)S(1)}, f32[8,8192]{1,0:T(8,128)S(1)}, u32[]{:S(2)}, u32[]{:S(2)}) %collective-permute-start.11) | collective-permute-done | bytes 262176 | tf_op jit(solution)/shard_map/ppermute | solution.py:118
  59.6 0.1 add_add_fusion
  59.7 1.1 multiply_subtract_fusion
  60.8 0.1 copy.15
  60.8 20.8 %all_to_all.10 = f32[32,2,4,128]{3,2,1,0:T(4,128)S(1)} all-to-all(f32[32,2,4,128]{3,2,1,0:T(4,128)S(1)} %copy.15), channel_id=1, replica_groups=mesh['y'=4,'far'=2,'x'=4,'core'=2,'dp'=8] {'y','x','core'}, dimensions={0} | all-to-all | bytes 262144 | tf_op jit(solution)/shard_map/all_to_all | solution.py:162
  81.7 15.1 %collective-permute-start.13 = (f32[2,4,128]{2,1,0:T(4,128)S(1)}, f32[2,4,128]{2,1,0:T(4,128)S(1)}, u32[]{:S(2)}, u32[]{:S(2)}) collective-permute-start(f32[2,4,128]{2,1,0:T(4,128)S(1)} %multiply_add_fusion.2), channel_id=1, source_target_pairs={{0,64},{64,0},{1,65},{65,1},{2,66},{66,2},{3,67},{67,3},{4,68},{68... | collective-permute-start | bytes 12296 | tf_op jit(solution)/shard_map/ppermute | solution.py:164
  96.8 1.0 collective-permute-done.13
  97.8 0.6 subtract_add_fusion
  98.4 12.1 %all_to_all.11 = f32[32,2,4,128]{3,2,1,0:T(4,128)S(1)} all-to-all(f32[32,2,4,128]{3,2,1,0:T(4,128)S(1)} %broadcast_in_dim.27), channel_id=1, replica_groups=mesh['y'=4,'far'=2,'x'=4,'core'=2,'dp'=8] {'y','x','core'}, dimensions={0} | all-to-all | bytes 262144 | tf_op jit(solution)/shard_map/all_to_all | solution.py:171
  110.6 0.8 fusion.2
  (36 shorter events, 0.5 us)
Async XLA Ops:
  0.7 8.6 %copy-start.3 = (f32[4,128]{1,0:T(4,128)S(1)}, f32[4,128]{1,0:T(4,128)}, u32[]{:S(2)}) copy-start(f32[4,128]{1,0:T(4,128)} %param.12) | copy-start | bytes 6148
  0.7 8.6 %copy-start.4 = (f32[4,128]{1,0:T(4,128)S(1)}, f32[4,128]{1,0:T(4,128)}, u32[]{:S(2)}) copy-start(f32[4,128]{1,0:T(4,128)} %param.13) | copy-start | bytes 6148
  3.5 7.7 %collective-permute-start = (f32[8,8192]{1,0:T(8,128)S(1)}, f32[8,8192]{1,0:T(8,128)S(1)}, u32[]{:S(2)}, u32[]{:S(2)}) collective-permute-start(f32[8,8192]{1,0:T(8,128)S(1)} %get-tuple-element.52), channel_id=1, source_target_pairs={{0,1},{1,2},{2,3},{3,4},{4,5},{5,6},{6,7},{8,9},{9,10},{10,11},{11... | collective-permute-start | bytes 786440 | tf_op jit(solution)/shard_map/ppermute | solution.py:100
  7.9 8.5 %collective-permute-start.2 = (f32[8,8192]{1,0:T(8,128)S(1)}, f32[8,8192]{1,0:T(8,128)S(1)}, u32[]{:S(2)}, u32[]{:S(2)}) collective-permute-start(f32[8,8192]{1,0:T(8,128)S(1)} %get-tuple-element.51), channel_id=1, source_target_pairs={{1,0},{2,1},{3,2},{4,3},{5,4},{6,5},{7,6},{9,8},{10,9},{11,10},{12... | collective-permute-start | bytes 786440 | tf_op jit(solution)/shard_map/ppermute | solution.py:101
  11.2 8.5 %collective-permute-start.1 = (f32[8,8192]{1,0:T(8,128)S(1)}, f32[8,8192]{1,0:T(8,128)S(1)}, u32[]{:S(2)}, u32[]{:S(2)}) collective-permute-start(f32[8,8192]{1,0:T(8,128)S(1)} %bitcast_add_fusion.5), channel_id=1, source_target_pairs={{0,1},{1,2},{8,9},{9,10},{16,17},{17,18},{24,25},{25,26},{32,33},{... | collective-permute-start | bytes 786440 | tf_op jit(solution)/shard_map/ppermute | solution.py:109
  16.5 8.1 %collective-permute-start.4 = (f32[8,8192]{1,0:T(8,128)S(1)}, f32[8,8192]{1,0:T(8,128)S(1)}, u32[]{:S(2)}, u32[]{:S(2)}) collective-permute-start(f32[8,8192]{1,0:T(8,128)S(1)} %bitcast_add_fusion.10), channel_id=1, source_target_pairs={{7,6},{6,5},{15,14},{14,13},{23,22},{22,21},{31,30},{30,29},{39,38... | collective-permute-start | bytes 786440 | tf_op jit(solution)/shard_map/ppermute | solution.py:112
  19.8 8.1 %collective-permute-start.3 = (f32[8,8192]{1,0:T(8,128)S(1)}, f32[8,8192]{1,0:T(8,128)S(1)}, u32[]{:S(2)}, u32[]{:S(2)}) collective-permute-start(f32[8,8192]{1,0:T(8,128)S(1)} %bitcast_add_fusion.6), channel_id=1, source_target_pairs={{0,1},{1,2},{2,3},{8,9},{9,10},{10,11},{16,17},{17,18},{18,19},{24... | collective-permute-start | bytes 786440 | tf_op jit(solution)/shard_map/ppermute | solution.py:109
  24.7 7.4 %collective-permute-start.6 = (f32[8,8192]{1,0:T(8,128)S(1)}, f32[8,8192]{1,0:T(8,128)S(1)}, u32[]{:S(2)}, u32[]{:S(2)}) collective-permute-start(f32[8,8192]{1,0:T(8,128)S(1)} %get-tuple-element.54), channel_id=1, source_target_pairs={{7,6},{6,5},{5,4},{15,14},{14,13},{13,12},{23,22},{22,21},{21,20},... | collective-permute-start | bytes 786440 | tf_op jit(solution)/shard_map/ppermute | solution.py:112
  28.0 7.4 %collective-permute-start.5 = (f32[8,8192]{1,0:T(8,128)S(1)}, f32[8,8192]{1,0:T(8,128)S(1)}, u32[]{:S(2)}, u32[]{:S(2)}) collective-permute-start(f32[8,8192]{1,0:T(8,128)S(1)} %bitcast_add_fusion.7), channel_id=1, source_target_pairs={{0,1},{1,2},{2,3},{3,4},{8,9},{9,10},{10,11},{11,12},{16,17},{17,1... | collective-permute-start | bytes 786440 | tf_op jit(solution)/shard_map/ppermute | solution.py:109
  32.1 27.5 %copy-start = (f32[4,8192]{1,0:T(4,128)S(1)}, f32[4,8192]{1,0:T(4,128)}, u32[]{:S(2)}) copy-start(f32[4,8192]{1,0:T(4,128)} %param.7) | copy-start | bytes 393220
  32.1 27.5 %copy-start.1 = (f32[4,8192]{1,0:T(4,128)S(1)}, f32[4,8192]{1,0:T(4,128)}, u32[]{:S(2)}) copy-start(f32[4,8192]{1,0:T(4,128)} %param.8) | copy-start | bytes 393220
  32.2 27.5 %copy-start.2 = (f32[4,8192]{1,0:T(4,128)S(1)}, f32[4,8192]{1,0:T(4,128)}, u32[]{:S(2)}) copy-start(f32[4,8192]{1,0:T(4,128)} %param.9) | copy-start | bytes 393220
  32.2 7.1 %collective-permute-start.8 = (f32[8,8192]{1,0:T(8,128)S(1)}, f32[8,8192]{1,0:T(8,128)S(1)}, u32[]{:S(2)}, u32[]{:S(2)}) collective-permute-start(f32[8,8192]{1,0:T(8,128)S(1)} %bitcast_add_fusion.1), channel_id=1, source_target_pairs={{7,6},{6,5},{5,4},{4,3},{15,14},{14,13},{13,12},{12,11},{23,22},{2... | collective-permute-start | bytes 786440 | tf_op jit(solution)/shard_map/ppermute | solution.py:112
  35.4 7.5 %collective-permute-start.7 = (f32[8,8192]{1,0:T(8,128)S(1)}, f32[8,8192]{1,0:T(8,128)S(1)}, u32[]{:S(2)}, u32[]{:S(2)}) collective-permute-start(f32[8,8192]{1,0:T(8,128)S(1)} %bitcast_add_fusion.8), channel_id=1, source_target_pairs={{0,1},{1,2},{2,3},{3,4},{4,5},{8,9},{9,10},{10,11},{11,12},{12,13}... | collective-permute-start | bytes 786440 | tf_op jit(solution)/shard_map/ppermute | solution.py:109
  39.3 8.7 %collective-permute-start.10 = (f32[8,8192]{1,0:T(8,128)S(1)}, f32[8,8192]{1,0:T(8,128)S(1)}, u32[]{:S(2)}, u32[]{:S(2)}) collective-permute-start(f32[8,8192]{1,0:T(8,128)S(1)} %bitcast_add_fusion), channel_id=1, source_target_pairs={{7,6},{6,5},{5,4},{4,3},{3,2},{15,14},{14,13},{13,12},{12,11},{11,... | collective-permute-start | bytes 786440 | tf_op jit(solution)/shard_map/ppermute | solution.py:112
  42.9 16.6 %collective-permute-start.9 = (f32[8,8192]{1,0:T(8,128)S(1)}, f32[8,8192]{1,0:T(8,128)S(1)}, u32[]{:S(2)}, u32[]{:S(2)}) collective-permute-start(f32[8,8192]{1,0:T(8,128)S(1)} %bitcast_add_fusion.9), channel_id=1, source_target_pairs={{0,2},{1,3},{2,4},{3,5},{4,6},{5,7},{8,10},{9,11},{10,12},{11,13},... | collective-permute-start | bytes 786440 | tf_op jit(solution)/shard_map/ppermute | solution.py:115
  48.1 11.5 %collective-permute-start.11 = (f32[8,8192]{1,0:T(8,128)S(1)}, f32[8,8192]{1,0:T(8,128)S(1)}, u32[]{:S(2)}, u32[]{:S(2)}) collective-permute-start(f32[8,8192]{1,0:T(8,128)S(1)} %bitcast_add_fusion.4), channel_id=1, source_target_pairs={{2,0},{3,1},{4,2},{5,3},{6,4},{7,5},{10,8},{11,9},{12,10},{13,11},... | collective-permute-start | bytes 786440 | tf_op jit(solution)/shard_map/ppermute | solution.py:118
  49.4 8.4 %collective-permute-start.12 = (f32[8,8192]{1,0:T(8,128)S(1)}, f32[8,8192]{1,0:T(8,128)S(1)}, u32[]{:S(2)}, u32[]{:S(2)}) collective-permute-start(f32[8,8192]{1,0:T(8,128)S(1)} %get-tuple-element.37), channel_id=1, source_target_pairs={{0,1},{7,6},{8,9},{15,14},{16,17},{23,22},{24,25},{31,30},{32,33},... | collective-permute-start | bytes 786440 | tf_op jit(solution)/shard_map/ppermute | solution.py:121
  81.7 16.1 %collective-permute-start.13 = (f32[2,4,128]{2,1,0:T(4,128)S(1)}, f32[2,4,128]{2,1,0:T(4,128)S(1)}, u32[]{:S(2)}, u32[]{:S(2)}) collective-permute-start(f32[2,4,128]{2,1,0:T(4,128)S(1)} %multiply_add_fusion.2), channel_id=1, source_target_pairs={{0,64},{64,0},{1,65},{65,1},{2,66},{66,2},{3,67},{67,3},{4,68},{68... | collective-permute-start | bytes 12296 | tf_op jit(solution)/shard_map/ppermute | solution.py:164
